TPU v7x, 32 devices: a whole 2x2x4 slice. The times are simulated.
32 devices in a mesh: row: 4 (over y, core), col: 4 (over z), depth: 2 (over x).
Axes of the slice: x: 2, y: 2, z: 4, core: 2. Of those that a mesh axis runs over, the one named last changes fastest.
Arguments:
- covariance: float32 [7168, 7168], P('row', 'col'), may hold values from -1 to 5, as said below
- iterate: float32 [7168, 7168], P('row', 'col'), may hold values from -1 to 1.5
Outputs:
- refreshed: float32 [7168, 4096], P(('row', 'depth'), 'col')
Inputs may be any that keep to these rules, and one draw needn't show every extreme that they name: `covariance`: symmetric.
All inputs are finite; a program needn't handle non-finite values.
Results may differ from a plain program's by a relative error of at most 0.00008.
Values sent between devices are 32-bit elements; how exact they have to be, the bound alone decides.
A program may use at most 128 MiB of HBM per device.

v0:
```python
import jax
import jax.numpy as jnp
from jax import lax
from jax.sharding import PartitionSpec as P

PERIOD = 896
SLAB = 512


def contraction_half(matrix, depth_pos, half_rows):
    tile_rows = matrix.shape[0]
    blocks = matrix.shape[1] // (2 * half_rows)
    shaped = matrix.reshape(tile_rows, blocks, 2, half_rows)
    picked = lax.dynamic_index_in_dim(shaped, depth_pos, 2, keepdims=False)
    return picked.reshape(tile_rows, blocks * half_rows)


def local(covariance, iterate):
    tile_rows = covariance.shape[0]
    tile_cols = covariance.shape[1]
    half_rows = tile_rows // 2
    depth_pos = lax.axis_index("depth")
    periods = tile_cols // PERIOD
    slab_width = periods * SLAB
    high = lax.Precision.HIGHEST
    slab_tile = iterate.reshape(tile_rows, periods, PERIOD)[:, :, :SLAB].reshape(
        tile_rows, slab_width
    )
    slab_half = lax.dynamic_slice_in_dim(slab_tile, depth_pos * half_rows, half_rows, 0)
    cov_half = contraction_half(covariance, depth_pos, half_rows)
    iter_half = contraction_half(iterate, depth_pos, half_rows)
    slab_whole = lax.all_gather(slab_half, "row", axis=0, tiled=True)
    rows_part = slab_whole
    partial_product = jnp.dot(
        lax.all_gather(cov_half, "col", axis=1, tiled=True),
        rows_part,
        precision=high,
        preferred_element_type=jnp.float32,
    )
    full_product = lax.psum(partial_product, "depth")
    product_share = lax.dynamic_slice_in_dim(full_product, depth_pos * half_rows, half_rows, 0)
    row_ids = (
        lax.axis_index("row") * tile_rows
        + depth_pos * half_rows
        + jnp.arange(half_rows, dtype=jnp.int32)
    )
    offsets = jnp.arange(slab_width, dtype=jnp.int32)
    col_ids = lax.axis_index("col") * tile_cols + offsets // SLAB * PERIOD + offsets % SLAB
    select = (row_ids[:, None] == col_ids[None, :]).astype(jnp.float32)
    residual_share = 2.0 * select - product_share
    residual_whole = lax.all_gather(residual_share, "row", axis=0, tiled=True)
    rows_part = residual_whole
    partial_result = jnp.dot(
        lax.all_gather(iter_half, "col", axis=1, tiled=True),
        rows_part,
        precision=high,
        preferred_element_type=jnp.float32,
    )
    return lax.psum_scatter(partial_result, "depth", scatter_dimension=0, tiled=True)


def solution(mesh):
    in_specs = (P("row", "col"), P("row", "col"))
    out_specs = P(("row", "depth"), "col")
    return jax.shard_map(local, mesh=mesh, in_specs=in_specs, out_specs=out_specs, check_vma=False)
```

profile of v0, /device:TPU:0, one launch (start us, length us, event | category | flops | bytes accessed | tf_op | source)
XLA Modules:
  0.0 1546.0 jit_solution(14806301566361281497)
XLA Ops:
  6.5 0.0 all-gather.7.cloned.1.call-start
  6.5 15.6 %reshape.51 = f32[1792,2,896]{2,1,0:T(2,128)} reshape(f32[1792,1792]{1,0:T(8,128)} %param.3) | data formatting | bytes 25690112 | tf_op jit(solution)/shard_map/reshape | solution.py:26
  22.1 0.0 slice-start
  22.1 3.1 slice-done
  25.2 4.8 copy.5
  30.0 4.4 constant_dynamic-slice_fusion
  34.3 0.0 all-gather.7.cloned.1.call-update
  34.4 0.0 all-gather.13.cloned.1.call-start
  34.4 15.8 %reshape.49 = f32[1792,1,2,896]{3,2,0,1:T(2,128)} reshape(f32[1792,1792]{1,0:T(8,128)} %param.2) | data formatting | bytes 25690112 | tf_op jit(solution)/shard_map/reshape | solution.py:13
  50.2 10.4 constant_dynamic-slice_fusion.1
  60.6 0.0 all-gather.13.cloned.1.call-update
  60.6 0.2 all-reduce.2.cloned.1.call-start
  60.8 70.4 %all-gather.7.cloned.1.call-done = f32[3584,1024]{1,0:T(8,128)} async-done(((f32[896,1024]{1,0:T(8,128)}), f32[3584,1024]{1,0:T(8,128)}) %all-gather.7.cloned.1.call-update) | async-done | bytes 14680080 | tf_op jit(solution)/shard_map/all_gather | solution.py:32
  131.2 435.2 %all-gather.13.cloned.1.call-done = f32[1792,1,1,3584]{3,2,0,1:T(1,128)} async-done(((f32[1792,1,1,896]{3,2,0,1:T(1,128)}), f32[1792,1,1,3584]{3,2,0,1:T(1,128)}) %all-gather.13.cloned.1.call-update) | async-done | bytes 25690128 | tf_op jit(solution)/shard_map/all_gather | solution.py:35
  566.5 90.5 %fusion = f32[1792,1024]{1,0:T(8,128)} fusion(f32[3584,1024]{1,0:T(8,128)} %all-gather.7.cloned.1.call-done, f32[1792,1,1,3584]{3,2,0,1:T(1,128)} %all-gather.13.cloned.1.call-done), kind=kOutput, calls=%fused_computation | convolution fusion | flops 78920024064 | bytes 47710208 | tf_op jit(solution)/shard_map/dot_general | solution.py:34
  657.0 0.0 all-reduce.2.cloned.1.call-update
  657.0 0.0 all-gather.11.cloned.1.call-start
  657.0 15.4 reshape.47
  672.4 9.8 constant_dynamic-slice_fusion.2
  682.2 0.0 all-gather.11.cloned.1.call-update
  682.3 0.0 all-gather.9.cloned.1.call-start
  682.3 148.8 %all-reduce.2.cloned.1.call-done = f32[1792,1024]{1,0:T(8,128)} async-done(((f32[1792,1024]{1,0:T(8,128)}), f32[1792,1024]{1,0:T(8,128)}) %all-reduce.2.cloned.1.call-update) | async-done | bytes 7340048 | tf_op jit(solution)/shard_map/psum | solution.py:40
  831.2 4.3 dynamic-slice_subtract_fusion
  835.5 0.0 all-gather.9.cloned.1.call-update
  835.5 0.3 reduce-scatter.2.cloned.1.call-start
  835.8 430.6 %all-gather.11.cloned.1.call-done = f32[1792,1,1,3584]{3,2,0,1:T(1,128)} async-done(((f32[1792,1,1,896]{3,2,0,1:T(1,128)}), f32[1792,1,1,3584]{3,2,0,1:T(1,128)}) %all-gather.11.cloned.1.call-update) | async-done | bytes 25690128 | tf_op jit(solution)/shard_map/all_gather | solution.py:54
  1266.4 93.7 %all-gather.9.cloned.1.call-done = f32[3584,1024]{1,0:T(8,128)} async-done(((f32[896,1024]{1,0:T(8,128)}), f32[3584,1024]{1,0:T(8,128)}) %all-gather.9.cloned.1.call-update) | async-done | bytes 14680080 | tf_op jit(solution)/shard_map/all_gather | solution.py:51
  1360.1 90.5 %fusion.3 = f32[1792,1024]{1,0:T(8,128)} fusion(f32[3584,1024]{1,0:T(8,128)} %all-gather.9.cloned.1.call-done, f32[1792,1,1,3584]{3,2,0,1:T(1,128)} %all-gather.11.cloned.1.call-done), kind=kOutput, calls=%fused_computation.3 | convolution fusion | flops 78920024064 | bytes 47710208 | tf_op jit(solution)/shard_map/dot_general | solution.py:53
  1450.6 0.0 reduce-scatter.2.cloned.1.call-update
  1450.6 88.6 %reduce-scatter.2.cloned.1.call-done = f32[896,1024]{1,0:T(8,128)} async-done(((f32[1792,1024]{1,0:T(8,128)}), f32[896,1024]{1,0:T(8,128)}) %reduce-scatter.2.cloned.1.call-update) | async-done | bytes 3670032 | tf_op jit(solution)/shard_map/reduce_scatter | solution.py:59
  (2 shorter events, 0.0 us)
Async XLA Ops:
  6.5 124.7 %all-gather.7.cloned.1.call-start = ((), (), s32[]{:S(2)}) async-start(), calls=%async_computation.1 | async-start | bytes 18350080 | tf_op jit(solution)/shard_map/all_gather | solution.py:32
  22.1 3.1 slice-start
  34.4 532.1 %all-gather.13.cloned.1.call-start = ((), (), s32[]{:S(2)}) async-start(), calls=%async_computation.6 | async-start | bytes 32112640 | tf_op jit(solution)/shard_map/all_gather | solution.py:35
  60.6 770.6 %all-reduce.2.cloned.1.call-start = ((), (), s32[]{:S(2)}) async-start(), calls=%async_computation.2 | async-start | bytes 14680064 | tf_op jit(solution)/shard_map/psum | solution.py:40
  657.0 609.4 %all-gather.11.cloned.1.call-start = ((), (), s32[]{:S(2)}) async-start(), calls=%async_computation.5 | async-start | bytes 32112640 | tf_op jit(solution)/shard_map/all_gather | solution.py:54
  682.3 677.8 %all-gather.9.cloned.1.call-start = ((), (), s32[]{:S(2)}) async-start(), calls=%async_computation.3 | async-start | bytes 18350080 | tf_op jit(solution)/shard_map/all_gather | solution.py:51
  835.5 703.7 %reduce-scatter.2.cloned.1.call-start = ((), (), s32[]{:S(2)}) async-start(), calls=%async_computation.4 | async-start | bytes 11010048 | tf_op jit(solution)/shard_map/reduce_scatter | solution.py:59
Sparse Core Ops, SparseCore 0:
  34.5 96.7 all-gather.6
  132.8 433.6 all-gather.12
  657.1 174.0 all-reduce.1
  832.7 433.6 all-gather.10
  1267.8 92.1 all-gather.8
  1450.7 88.4 reduce-scatter.1
where the time goes:
time: 1550 us
  waiting for transfers between devices  1270 us (82%)
  matrix products  181 us (12%)
  local copies, waits for them, and re-layouts  79.1 us (5%)
    all_gather x1, waiting for transfers between devices, local(): lax.all_gather(cov_half, 'col', axis=1, tiled=True)  435 us
    all_gather x1, waiting for transfers between devices, local(): lax.all_gather(iter_half, 'col', axis=1, tiled=True)  431 us
    psum x1, waiting for transfers between devices, local(): full_product = lax.psum(partial_product, 'depth')  149 us
    all_gather x1, waiting for transfers between devices, local(): residual_whole = lax.all_gather(residual_share, 'row', axis=0, tiled=True)  93.7 us
    dot_general x1, matrix products, local(): jnp.dot(lax.all_gather(cov_half, 'col', axis=1, tiled=True), rows_part, p...  90.5 us
    dot_general x1, matrix products, local(): jnp.dot(lax.all_gather(iter_half, 'col', axis=1, tiled=True), rows_part,...  90.5 us
    reduce_scatter x1, waiting for transfers between devices, local(): lax.psum_scatter(partial_result, 'depth', scatter_dimension=0, tiled=True)  88.6 us
    all_gather x1, waiting for transfers between devices, local(): slab_whole = lax.all_gather(slab_half, 'row', axis=0, tiled=True)  70.4 us
  transfers between devices with their start and end apart: 6, of which 6 were waited for; matrix products, arithmetic and copies ran while one was open for 4% of the time, Pallas kernels for 0%

commit v1 on v0

v1 whole, which is shorter than its diff:
```python
import jax
import jax.numpy as jnp
from jax import lax
from jax.sharding import PartitionSpec as P

PERIOD = 896
SLAB = 512
CHUNK = 64
HIGH = lax.Precision.HIGH


def column_of(offset):
    return offset // SLAB * PERIOD + offset % SLAB


def halves(pick_second, array, axis):
    first, second = jnp.split(array, 2, axis=axis)
    return jnp.where(pick_second, second, first), jnp.where(pick_second, first, second)


def gather_line(block, size):
    right, left = [block], [block]
    for step in range(size - 1):
        right.append(
            lax.ppermute(right[-1], "col", [(i, i + 1) for i in range(step, size - 1)])
        )
        left.append(
            lax.ppermute(left[-1], "col", [(i + 1, i) for i in range(size - 1 - step)])
        )
    slots = [block]
    for slot in range(1, size):
        slots.append(left[slot] + right[size - slot])
    return jnp.concatenate(slots, axis=0)


def sum_rows(part, size):
    core = lax.axis_index("row") % 2
    kept, given = halves(core == 1, part, 0)
    cores = [(i, i ^ 1) for i in range(size)]
    kept = kept + lax.ppermute(given, "row", cores)
    bit = 2
    while bit < size:
        kept = kept + lax.ppermute(kept, "row", [(i, i ^ bit) for i in range(size)])
        bit *= 2
    other = lax.ppermute(kept, "row", cores)
    return jnp.where(
        core == 0,
        jnp.concatenate([kept, other], axis=0),
        jnp.concatenate([other, kept], axis=0),
    )


def scatter_line(part, size):
    slots = jnp.split(part, size, axis=0)
    right, left = None, None
    for step in range(size - 1):
        ahead = slots[size - 1 - step]
        behind = slots[step + 1]
        ahead = ahead if right is None else ahead + right
        behind = behind if left is None else behind + left
        right = lax.ppermute(ahead, "col", [(i, i + 1) for i in range(step + 1)])
        left = lax.ppermute(behind, "col", [(size - 1 - i, size - 2 - i) for i in range(step + 1)])
    return slots[0] + right + left


def solution(mesh):
    rows, cols = mesh.shape["row"], mesh.shape["col"]

    def local(covariance, iterate):
        tile_cols = covariance.shape[1]
        half = tile_cols // PERIOD * SLAB // 2
        chunk = min(CHUNK, half)
        depth = lax.axis_index("depth")
        own, peer = [], []
        gathered = []
        for start in range(0, half, chunk):
            near, far = column_of(start), column_of(half + start)
            window = jnp.where(
                depth == 0, iterate[:, near : near + chunk], iterate[:, far : far + chunk]
            ).T
            gathered.append(gather_line(window, cols))
        for number, start in enumerate(range(0, half, chunk)):
            near, far = column_of(start), column_of(half + start)
            part = jnp.dot(
                gathered[number],
                covariance,
                precision=HIGH,
                preferred_element_type=jnp.float32,
            )
            product = sum_rows(part, rows)
            here = jnp.where(depth == 0, near, far)
            shape = product.shape
            slot_row = lax.broadcasted_iota(jnp.int32, shape, 0)
            place = lax.broadcasted_iota(jnp.int32, shape, 1)
            select = (slot_row < chunk) & (place == here + slot_row)
            residual = jnp.where(select, 2.0, 0.0) - product
            part = lax.dot_general(
                residual,
                iterate,
                (((1,), (1,)), ((), ())),
                precision=HIGH,
                preferred_element_type=jnp.float32,
            )
            result = scatter_line(part, cols)
            kept, given = halves(depth == 1, result, 1)
            own.append(kept)
            peer.append(lax.ppermute(given, "depth", [(0, 1), (1, 0)]))
        first = jnp.where(depth == 0, jnp.concatenate(own, 0), jnp.concatenate(peer, 0))
        second = jnp.where(depth == 0, jnp.concatenate(peer, 0), jnp.concatenate(own, 0))
        return jnp.concatenate([first, second], axis=0).T

    in_specs = (P("row", "col"), P("row", "col"))
    out_specs = P(("row", "depth"), "col")
    return jax.shard_map(local, mesh=mesh, in_specs=in_specs, out_specs=out_specs, check_vma=False)
```

time: 1550 us -> 899 us (0.58)
  waiting for transfers between devices: 1270 us -> 279 us
  starting transfers between devices: 0.61 us -> 328 us
  other arithmetic: 4.31 us -> 79.2 us
  matrix products: 181 us -> 140 us
  local copies, waits for them, and re-layouts: 79.1 us -> 57.4 us
    all_gather x4 -> x0, waiting for transfers between devices: 1030 us -> none  [the longest x1 435 us: local(): lax.all_gather(cov_half, 'col', axis=1, tiled=True)]
    ppermute x0 -> x128, starting transfers between devices: none -> 328 us  [the longest x24 125 us: scatter_line(): right = lax.ppermute(ahead, 'col', [(i, i + 1) for i in range(step + 1)])]
    ppermute x0 -> x128, waiting for transfers between devices: none -> 279 us  [the longest x8 101 us: sum_rows(): kept = kept + lax.ppermute(kept, 'row', [(i, i ^ bit) for i in range(size)])]
    psum x1 -> x0, waiting for transfers between devices: 149 us -> none  [local(): full_product = lax.psum(partial_product, 'depth')]
    reduce_scatter x1 -> x0, waiting for transfers between devices: 88.6 us -> none  [local(): lax.psum_scatter(partial_result, 'depth', scatter_dimension=0, tiled=True)]
    add x2 -> x72, other arithmetic: 0.01 us -> 64.6 us  [the longest x24 37.4 us: gather_line(): slots.append(left[slot] + right[size - slot])]
    reshape x3 -> x0, local copies, waits for them, and re-layouts: 46.7 us -> none  [the longest x2 31.1 us: contraction_half(): shaped = matrix.reshape(tile_rows, blocks, 2, half_rows)]
    dot_general x2 -> x16, matrix products: 181 us -> 140 us  [the longest x8 70.9 us: local(): lax.dot_general(residual, iterate, (((1,), (1,)), ((), ())), precision=HI...]
  transfers between devices with their start and end apart: 6 -> 128, of which waited for: 6 -> 45; matrix products, arithmetic and copies ran while one was open for 4% -> 28% of each run, Pallas kernels for 0% -> 0%
where the time goes in v1:
time: 899 us; the launch traced here: 886 us
  starting transfers between devices  328 us (36%)
  waiting for transfers between devices  279 us (31%)
  matrix products  140 us (16%)
  other arithmetic  79.2 us (9%)
  local copies, waits for them, and re-layouts  57.4 us (6%)
    ppermute x24, starting transfers between devices, scatter_line(): right = lax.ppermute(ahead, 'col', [(i, i + 1) for i in range(step + 1)])  125 us
    ppermute x8, waiting for transfers between devices, sum_rows(): kept = kept + lax.ppermute(kept, 'row', [(i, i ^ bit) for i in range(size)])  101 us
    ppermute x24, waiting for transfers between devices, gather_line(): lax.ppermute(left[-1], 'col', [(i + 1, i) for i in range(size - 1 - step)])  96.5 us
    dot_general x8, matrix products, local(): lax.dot_general(residual, iterate, (((1,), (1,)), ((), ())), precision=HI...  70.9 us
    dot_general x8, matrix products, local(): jnp.dot(gathered[number], covariance, precision=HIGH, preferred_element_t...  69 us
    ppermute x24, starting transfers between devices, gather_line(): lax.ppermute(right[-1], 'col', [(i, i + 1) for i in range(step, size - 1)])  53.3 us
    ppermute x24, waiting for transfers between devices, scatter_line(): right = lax.ppermute(ahead, 'col', [(i, i + 1) for i in range(step + 1)])  45.3 us
    ppermute x8, starting transfers between devices, sum_rows(): kept = kept + lax.ppermute(kept, 'row', [(i, i ^ bit) for i in range(size)])  43.2 us
  transfers between devices with their start and end apart: 128, of which 45 were waited for; matrix products, arithmetic and copies ran while one was open for 28% of the time, Pallas kernels for 0%

profile of v1, /device:TPU:0, one launch (start us, length us, event | category | flops | bytes accessed | tf_op | source)
XLA Modules:
  0.0 886.1 jit_solution(3292464426455951519)
XLA Ops:
  0.0 12.4 %fusion.232 = (f32[1792,64]{1,0:T(8,128)S(1)}, f32[1792,64]{1,0:T(8,128)S(1)}, f32[1792,64]{1,0:T(8,128)S(1)}, f32[1792,64]{1,0:T(8,128)}, f32[1792,64]{1,0:T(8,...) fusion(f32[1792,1792]{1,0:T(8,128)} %param.3), kind=kLoop, calls=%fused_computation.332 | loop fusion | bytes 14680064 | tf_op jit(solution)/shard_map/slice | solution.py:79
  110.5 7.3 collective-permute-done.90
  120.5 7.1 collective-permute-done.105
  130.4 7.2 collective-permute-done.19
  139.6 7.8 collective-permute-done.4
  150.1 7.1 collective-permute-done.34
  159.9 7.0 collective-permute-done.49
  169.7 7.2 collective-permute-done.64
  178.9 7.8 collective-permute-done.79
  188.7 7.8 collective-permute-done.94
  199.3 7.1 collective-permute-done.109
  238.7 9.7 %fusion.16 = f32[256,1792]{1,0:T(8,128)S(1)} fusion(f32[1792,1792]{1,0:T(8,128)} %param.2, f32[64,1792]{1,0:T(8,128)S(1)} %add.349, f32[64,1792]{1,0:T(8,128)S(1)} %add.348, f32[64,1792]{1,0:T(8,128)S(1)} %add.347, f32[64,1792]{1,0:T(8,128)} %select_bitcast_fusion.6), kind=kOutput, calls=%fused_computation.17 | convolution fusion | flops 4933877760 | bytes 16515072 | tf_op jit(solution)/shard_map/dot_general | solution.py:84
  251.6 7.7 fusion
  263.1 7.7 fusion.32
  274.0 7.7 fusion.48
  285.2 8.1 fusion.64
  300.7 9.2 %fusion.80 = f32[256,1792]{1,0:T(8,128)} fusion(f32[1792,1792]{1,0:T(8,128)S(1)} %bitcast.37, f32[64,1792]{1,0:T(8,128)} %add.401, f32[64,1792]{1,0:T(8,128)} %add.400, f32[64,1792]{1,0:T(8,128)} %add.399, f32[64,1792]{1,0:T(8,128)S(1)} %select_bitcast_fusion.2), kind=kOutput, calls=%fused_computation.81 | convolution fusion | flops 4933877760 | bytes 16515072 | tf_op jit(solution)/shard_map/dot_general | solution.py:84
  316.2 9.6 %fusion.96 = f32[256,1792]{1,0:T(8,128)} fusion(f32[1792,1792]{1,0:T(8,128)S(1)} %bitcast.37, f32[64,1792]{1,0:T(8,128)} %add.414, f32[64,1792]{1,0:T(8,128)} %add.413, f32[64,1792]{1,0:T(8,128)} %add.412, f32[64,1792]{1,0:T(8,128)S(1)} %copy-done.23), kind=kOutput, calls=%fused_computation.97 | convolution fusion | flops 4933877760 | bytes 16515072 | tf_op jit(solution)/shard_map/dot_general | solution.py:84
  326.9 12.5 %collective-permute-start.51 = (f32[128,1792]{1,0:T(8,128)}, f32[128,1792]{1,0:T(8,128)}, u32[]{:S(2)}, u32[]{:S(2)}) collective-permute-start(f32[128,1792]{1,0:T(8,128)} %slice_select_fusion.4), channel_id=1, source_target_pairs={{0,8},{8,0},{16,24},{24,16},{1,9},{9,1},{17,25},{25,17},{2,10},{10... | collective-permute-start | bytes 2752520 | tf_op jit(solution)/shard_map/ppermute | solution.py:40
  349.9 9.2 %fusion.112 = f32[256,1792]{1,0:T(8,128)} fusion(f32[1792,1792]{1,0:T(8,128)S(1)} %bitcast.37, f32[64,1792]{1,0:T(8,128)} %add.427, f32[64,1792]{1,0:T(8,128)} %add.426, f32[64,1792]{1,0:T(8,128)} %add.425, f32[64,1792]{1,0:T(8,128)S(1)} %copy-done.25), kind=kOutput, calls=%fused_computation.113 | convolution fusion | flops 4933877760 | bytes 16515072 | tf_op jit(solution)/shard_map/dot_general | solution.py:84
  420.2 15.3 %collective-permute-done.37 = f32[128,1792]{1,0:T(8,128)S(1)} collective-permute-done((f32[128,1792]{1,0:T(8,128)S(1)}, f32[128,1792]{1,0:T(8,128)S(1)}, u32[]{:S(2)}, u32[]{:S(2)}) %collective-permute-start.37) | collective-permute-done | bytes 917536 | tf_op jit(solution)/shard_map/ppermute | solution.py:43
  439.9 15.3 %collective-permute-done.52 = f32[128,1792]{1,0:T(8,128)S(1)} collective-permute-done((f32[128,1792]{1,0:T(8,128)S(1)}, f32[128,1792]{1,0:T(8,128)S(1)}, u32[]{:S(2)}, u32[]{:S(2)}) %collective-permute-start.52) | collective-permute-done | bytes 917536 | tf_op jit(solution)/shard_map/ppermute | solution.py:43
  459.8 15.1 %collective-permute-done.67 = f32[128,1792]{1,0:T(8,128)} collective-permute-done((f32[128,1792]{1,0:T(8,128)}, f32[128,1792]{1,0:T(8,128)}, u32[]{:S(2)}, u32[]{:S(2)}) %collective-permute-start.67) | collective-permute-done | bytes 917536 | tf_op jit(solution)/shard_map/ppermute | solution.py:43
  476.6 17.9 %collective-permute-done.82 = f32[128,1792]{1,0:T(8,128)} collective-permute-done((f32[128,1792]{1,0:T(8,128)S(1)}, f32[128,1792]{1,0:T(8,128)}, u32[]{:S(2)}, u32[]{:S(2)}) %collective-permute-start.82) | collective-permute-done | bytes 917536 | tf_op jit(solution)/shard_map/ppermute | solution.py:43
  495.8 18.4 %collective-permute-done.97 = f32[128,1792]{1,0:T(8,128)} collective-permute-done((f32[128,1792]{1,0:T(8,128)}, f32[128,1792]{1,0:T(8,128)}, u32[]{:S(2)}, u32[]{:S(2)}) %collective-permute-start.97) | collective-permute-done | bytes 917536 | tf_op jit(solution)/shard_map/ppermute | solution.py:43
  521.1 12.3 %collective-permute-done.112 = f32[128,1792]{1,0:T(8,128)} collective-permute-done((f32[128,1792]{1,0:T(8,128)}, f32[128,1792]{1,0:T(8,128)}, u32[]{:S(2)}, u32[]{:S(2)}) %collective-permute-start.112) | collective-permute-done | bytes 917536 | tf_op jit(solution)/shard_map/ppermute | solution.py:43
  540.8 12.9 %fusion.25 = f32[256,1792]{1,0:T(8,128)S(1)} fusion(f32[1792,1792]{1,0:T(8,128)} %param.3, f32[128,1792]{1,0:T(8,128)} %collective-permute-done.23, f32[128,1792]{1,0:T(8,128)} %add.351, s32[256]{0:T(256)S(1)} %iota_add_fusion.6, pred[256]{0:T(512)(128)(4,1)S(1)} %iota_compare_fusion.8, pred[]{:T(512)S(6)} %eq.36), kind=kOutput, calls=%fused_computation.27 | convolution fusion | flops 4935712768 | bytes 16516353 | tf_op jit(solution)/shard_map/dot_general | solution.py:97
  555.8 8.0 fusion.9
  564.2 9.0 %fusion.41 = f32[256,1792]{1,0:T(8,128)S(1)} fusion(f32[1792,1792]{1,0:T(8,128)S(1)} %bitcast.35, f32[128,1792]{1,0:T(8,128)} %collective-permute-done.38, f32[128,1792]{1,0:T(8,128)} %add.364, s32[256]{0:T(256)S(1)} %iota_add_fusion.5, pred[256]{0:T(512)(128)(4,1)S(1)} %iota_compare_fusion.8, pred[]{:T(512)S(6)} %eq.36), kind=kOutput, calls=%fused_computation.43 | convolution fusion | flops 4935712768 | bytes 16516353 | tf_op jit(solution)/shard_map/dot_general | solution.py:97
  579.9 8.0 fusion.57
  589.5 8.0 fusion.73
  601.4 8.0 fusion.89
  611.6 8.6 fusion.105
  624.3 8.6 fusion.121
  648.1 8.3 collective-permute-done.69
  676.0 7.7 collective-permute-start.10
  686.5 9.0 %collective-permute-start.40 = (f32[64,1792]{1,0:T(8,128)S(1)}, f32[64,1792]{1,0:T(8,128)S(1)}, u32[]{:S(2)}, u32[]{:S(2)}) collective-permute-start(f32[64,1792]{1,0:T(8,128)S(1)} %get-tuple-element.55), channel_id=1, source_target_pairs={{0,2},{2,4},{1,3},{3,5},{8,10},{10,12},{9,11},{11,13},{16,18},{18,... | collective-permute-start | bytes 1376264 | tf_op jit(solution)/shard_map/ppermute | solution.py:61
  696.4 7.2 collective-permute-start.55
  706.2 7.2 collective-permute-start.70
  716.0 7.2 collective-permute-start.85
  725.8 7.2 collective-permute-start.100
  735.7 7.2 collective-permute-start.115
  745.5 7.2 collective-permute-start.26
  755.9 7.1 collective-permute-start.11
  765.8 7.1 collective-permute-start.41
  773.0 11.2 %collective-permute-done.11 = f32[64,1792]{1,0:T(8,128)S(1)} collective-permute-done((f32[64,1792]{1,0:T(8,128)S(1)}, f32[64,1792]{1,0:T(8,128)S(1)}, u32[]{:S(2)}, u32[]{:S(2)}) %collective-permute-start.11) | collective-permute-done | bytes 458784 | tf_op jit(solution)/shard_map/ppermute | solution.py:61
  791.9 10.6 %collective-permute-start.71 = (f32[64,1792]{1,0:T(8,128)S(1)}, f32[64,1792]{1,0:T(8,128)S(1)}, u32[]{:S(2)}, u32[]{:S(2)}) collective-permute-start(f32[64,1792]{1,0:T(8,128)S(1)} %get-tuple-element.41), channel_id=1, source_target_pairs={{0,2},{2,4},{4,6},{1,3},{3,5},{5,7},{8,10},{10,12},{12,14},{9,11},... | collective-permute-start | bytes 1376264 | tf_op jit(solution)/shard_map/ppermute | solution.py:61
  842.9 7.0 collective-permute-start.123
  (513 shorter events, 439.9 us)
Async XLA Ops:
  16.9 46.0 %collective-permute-start.16 = (f32[64,1792]{1,0:T(8,128)}, f32[64,1792]{1,0:T(8,128)}, u32[]{:S(2)}, u32[]{:S(2)}) collective-permute-start(f32[64,1792]{1,0:T(8,128)} %select_bitcast_fusion.6), channel_id=1, source_target_pairs={{0,2},{2,4},{4,6},{1,3},{3,5},{5,7},{8,10},{10,12},{12,14},{9,11},... | collective-permute-start | bytes 1376264 | tf_op jit(solution)/shard_map/ppermute | solution.py:25
  22.6 41.6 %collective-permute-start.15 = (f32[64,1792]{1,0:T(8,128)}, f32[64,1792]{1,0:T(8,128)}, u32[]{:S(2)}, u32[]{:S(2)}) collective-permute-start(f32[64,1792]{1,0:T(8,128)} %select_bitcast_fusion.6), channel_id=1, source_target_pairs={{2,0},{4,2},{6,4},{3,1},{5,3},{7,5},{10,8},{12,10},{14,12},{11,9},... | collective-permute-start | bytes 1376264 | tf_op jit(solution)/shard_map/ppermute | solution.py:28
  28.5 40.3 %collective-permute-start.1 = (f32[64,1792]{1,0:T(8,128)}, f32[64,1792]{1,0:T(8,128)}, u32[]{:S(2)}, u32[]{:S(2)}) collective-permute-start(f32[64,1792]{1,0:T(8,128)} %select_bitcast_fusion.7), channel_id=1, source_target_pairs={{0,2},{2,4},{4,6},{1,3},{3,5},{5,7},{8,10},{10,12},{12,14},{9,11},... | collective-permute-start | bytes 1376264 | tf_op jit(solution)/shard_map/ppermute | solution.py:25
  33.8 36.3 %collective-permute-start = (f32[64,1792]{1,0:T(8,128)}, f32[64,1792]{1,0:T(8,128)}, u32[]{:S(2)}, u32[]{:S(2)}) collective-permute-start(f32[64,1792]{1,0:T(8,128)} %select_bitcast_fusion.7), channel_id=1, source_target_pairs={{2,0},{4,2},{6,4},{3,1},{5,3},{7,5},{10,8},{12,10},{14,12},{11,9},... | collective-permute-start | bytes 1376264 | tf_op jit(solution)/shard_map/ppermute | solution.py:28
  39.6 35.2 %collective-permute-start.31 = (f32[64,1792]{1,0:T(8,128)}, f32[64,1792]{1,0:T(8,128)}, u32[]{:S(2)}, u32[]{:S(2)}) collective-permute-start(f32[64,1792]{1,0:T(8,128)} %select_bitcast_fusion.5), channel_id=1, source_target_pairs={{0,2},{2,4},{4,6},{1,3},{3,5},{5,7},{8,10},{10,12},{12,14},{9,11},... | collective-permute-start | bytes 1376264 | tf_op jit(solution)/shard_map/ppermute | solution.py:25
  187.4 35.6 %collective-permute-start.20 = (f32[64,1792]{1,0:T(8,128)}, f32[64,1792]{1,0:T(8,128)}, u32[]{:S(2)}, u32[]{:S(2)}) collective-permute-start(f32[64,1792]{1,0:T(8,128)} %collective-permute-done.19), channel_id=1, source_target_pairs={{2,0},{3,1},{10,8},{11,9},{18,16},{19,17},{26,24},{27,25}} | collective-permute-start | bytes 1376264 | tf_op jit(solution)/shard_map/ppermute | solution.py:28
  196.5 29.3 %collective-permute-start.3 = (f32[64,1792]{1,0:T(8,128)}, f32[64,1792]{1,0:T(8,128)}, u32[]{:S(2)}, u32[]{:S(2)}) collective-permute-start(f32[64,1792]{1,0:T(8,128)} %collective-permute-done.2), channel_id=1, source_target_pairs={{4,6},{5,7},{12,14},{13,15},{20,22},{21,23},{28,30},{29,31}} | collective-permute-start | bytes 1376264 | tf_op jit(solution)/shard_map/ppermute | solution.py:25
  198.0 30.6 %collective-permute-start.5 = (f32[64,1792]{1,0:T(8,128)}, f32[64,1792]{1,0:T(8,128)}, u32[]{:S(2)}, u32[]{:S(2)}) collective-permute-start(f32[64,1792]{1,0:T(8,128)} %collective-permute-done.4), channel_id=1, source_target_pairs={{2,0},{3,1},{10,8},{11,9},{18,16},{19,17},{26,24},{27,25}} | collective-permute-start | bytes 1376264 | tf_op jit(solution)/shard_map/ppermute | solution.py:28
  225.9 33.5 %collective-permute-start.50 = (f32[64,1792]{1,0:T(8,128)S(1)}, f32[64,1792]{1,0:T(8,128)}, u32[]{:S(2)}, u32[]{:S(2)}) collective-permute-start(f32[64,1792]{1,0:T(8,128)S(1)} %copy-done.63), channel_id=1, source_target_pairs={{2,0},{3,1},{10,8},{11,9},{18,16},{19,17},{26,24},{27,25}} | collective-permute-start | bytes 1376264 | tf_op jit(solution)/shard_map/ppermute | solution.py:28
  228.6 42.2 %collective-permute-start.63 = (f32[64,1792]{1,0:T(8,128)}, f32[64,1792]{1,0:T(8,128)}, u32[]{:S(2)}, u32[]{:S(2)}) collective-permute-start(f32[64,1792]{1,0:T(8,128)} %collective-permute-done.62), channel_id=1, source_target_pairs={{4,6},{5,7},{12,14},{13,15},{20,22},{21,23},{28,30},{29,31}} | collective-permute-start | bytes 1376264 | tf_op jit(solution)/shard_map/ppermute | solution.py:25
  231.3 50.4 %collective-permute-start.65 = (f32[64,1792]{1,0:T(8,128)}, f32[64,1792]{1,0:T(8,128)}, u32[]{:S(2)}, u32[]{:S(2)}) collective-permute-start(f32[64,1792]{1,0:T(8,128)} %collective-permute-done.64), channel_id=1, source_target_pairs={{2,0},{3,1},{10,8},{11,9},{18,16},{19,17},{26,24},{27,25}} | collective-permute-start | bytes 1376264 | tf_op jit(solution)/shard_map/ppermute | solution.py:28
  235.9 58.6 %collective-permute-start.78 = (f32[64,1792]{1,0:T(8,128)}, f32[64,1792]{1,0:T(8,128)}, u32[]{:S(2)}, u32[]{:S(2)}) collective-permute-start(f32[64,1792]{1,0:T(8,128)} %collective-permute-done.77), channel_id=1, source_target_pairs={{4,6},{5,7},{12,14},{13,15},{20,22},{21,23},{28,30},{29,31}} | collective-permute-start | bytes 1376264 | tf_op jit(solution)/shard_map/ppermute | solution.py:25
  248.5 50.4 %collective-permute-start.80 = (f32[64,1792]{1,0:T(8,128)}, f32[64,1792]{1,0:T(8,128)}, u32[]{:S(2)}, u32[]{:S(2)}) collective-permute-start(f32[64,1792]{1,0:T(8,128)} %collective-permute-done.79), channel_id=1, source_target_pairs={{2,0},{3,1},{10,8},{11,9},{18,16},{19,17},{26,24},{27,25}} | collective-permute-start | bytes 1376264 | tf_op jit(solution)/shard_map/ppermute | solution.py:28
  259.3 51.5 %collective-permute-start.93 = (f32[64,1792]{1,0:T(8,128)}, f32[64,1792]{1,0:T(8,128)}, u32[]{:S(2)}, u32[]{:S(2)}) collective-permute-start(f32[64,1792]{1,0:T(8,128)} %collective-permute-done.92), channel_id=1, source_target_pairs={{4,6},{5,7},{12,14},{13,15},{20,22},{21,23},{28,30},{29,31}} | collective-permute-start | bytes 1376264 | tf_op jit(solution)/shard_map/ppermute | solution.py:25
  270.8 43.5 %collective-permute-start.95 = (f32[64,1792]{1,0:T(8,128)}, f32[64,1792]{1,0:T(8,128)}, u32[]{:S(2)}, u32[]{:S(2)}) collective-permute-start(f32[64,1792]{1,0:T(8,128)} %collective-permute-done.94), channel_id=1, source_target_pairs={{2,0},{3,1},{10,8},{11,9},{18,16},{19,17},{26,24},{27,25}} | collective-permute-start | bytes 1376264 | tf_op jit(solution)/shard_map/ppermute | solution.py:28
  281.7 45.2 %collective-permute-start.108 = (f32[64,1792]{1,0:T(8,128)}, f32[64,1792]{1,0:T(8,128)}, u32[]{:S(2)}, u32[]{:S(2)}) collective-permute-start(f32[64,1792]{1,0:T(8,128)} %copy-done.60), channel_id=1, source_target_pairs={{4,6},{5,7},{12,14},{13,15},{20,22},{21,23},{28,30},{29,31}} | collective-permute-start | bytes 1376264 | tf_op jit(solution)/shard_map/ppermute | solution.py:25
  294.4 47.9 %collective-permute-start.110 = (f32[64,1792]{1,0:T(8,128)}, f32[64,1792]{1,0:T(8,128)}, u32[]{:S(2)}, u32[]{:S(2)}) collective-permute-start(f32[64,1792]{1,0:T(8,128)} %collective-permute-done.109), channel_id=1, source_target_pairs={{2,0},{3,1},{10,8},{11,9},{18,16},{19,17},{26,24},{27,25}} | collective-permute-start | bytes 1376264 | tf_op jit(solution)/shard_map/ppermute | solution.py:28
  298.8 62.4 %collective-permute-start.21 = (f32[128,1792]{1,0:T(8,128)}, f32[128,1792]{1,0:T(8,128)}, u32[]{:S(2)}, u32[]{:S(2)}) collective-permute-start(f32[128,1792]{1,0:T(8,128)} %slice_select_fusion.6), channel_id=1, source_target_pairs={{0,8},{8,0},{16,24},{24,16},{1,9},{9,1},{17,25},{25,17},{2,10},{10... | collective-permute-start | bytes 2752520 | tf_op jit(solution)/shard_map/ppermute | solution.py:40
  310.9 53.2 %collective-permute-start.6 = (f32[128,1792]{1,0:T(8,128)}, f32[128,1792]{1,0:T(8,128)}, u32[]{:S(2)}, u32[]{:S(2)}) collective-permute-start(f32[128,1792]{1,0:T(8,128)} %slice_select_fusion.7), channel_id=1, source_target_pairs={{0,8},{8,0},{16,24},{24,16},{1,9},{9,1},{17,25},{25,17},{2,10},{10... | collective-permute-start | bytes 2752520 | tf_op jit(solution)/shard_map/ppermute | solution.py:40
  314.3 51.4 %collective-permute-start.36 = (f32[128,1792]{1,0:T(8,128)}, f32[128,1792]{1,0:T(8,128)}, u32[]{:S(2)}, u32[]{:S(2)}) collective-permute-start(f32[128,1792]{1,0:T(8,128)} %slice_select_fusion.5), channel_id=1, source_target_pairs={{0,8},{8,0},{16,24},{24,16},{1,9},{9,1},{17,25},{25,17},{2,10},{10... | collective-permute-start | bytes 2752520 | tf_op jit(solution)/shard_map/ppermute | solution.py:40
  326.9 40.5 %collective-permute-start.51 = (f32[128,1792]{1,0:T(8,128)}, f32[128,1792]{1,0:T(8,128)}, u32[]{:S(2)}, u32[]{:S(2)}) collective-permute-start(f32[128,1792]{1,0:T(8,128)} %slice_select_fusion.4), channel_id=1, source_target_pairs={{0,8},{8,0},{16,24},{24,16},{1,9},{9,1},{17,25},{25,17},{2,10},{10... | collective-permute-start | bytes 2752520 | tf_op jit(solution)/shard_map/ppermute | solution.py:40
  342.3 32.2 %collective-permute-start.66 = (f32[128,1792]{1,0:T(8,128)}, f32[128,1792]{1,0:T(8,128)}, u32[]{:S(2)}, u32[]{:S(2)}) collective-permute-start(f32[128,1792]{1,0:T(8,128)} %slice_select_fusion.3), channel_id=1, source_target_pairs={{0,8},{8,0},{16,24},{24,16},{1,9},{9,1},{17,25},{25,17},{2,10},{10... | collective-permute-start | bytes 2752520 | tf_op jit(solution)/shard_map/ppermute | solution.py:40
  365.6 29.7 %collective-permute-start.111 = (f32[128,1792]{1,0:T(8,128)S(1)}, f32[128,1792]{1,0:T(8,128)S(1)}, u32[]{:S(2)}, u32[]{:S(2)}) collective-permute-start(f32[128,1792]{1,0:T(8,128)S(1)} %slice_select_fusion), channel_id=1, source_target_pairs={{0,8},{8,0},{16,24},{24,16},{1,9},{9,1},{17,25},{25,17},{2,10},{10... | collective-permute-start | bytes 2752520 | tf_op jit(solution)/shard_map/ppermute | solution.py:40
  367.4 34.8 %collective-permute-start.22 = (f32[128,1792]{1,0:T(8,128)S(1)}, f32[128,1792]{1,0:T(8,128)S(1)}, u32[]{:S(2)}, u32[]{:S(2)}) collective-permute-start(f32[128,1792]{1,0:T(8,128)S(1)} %select_add_fusion.6), channel_id=1, source_target_pairs={{0,16},{8,24},{16,0},{24,8},{1,17},{9,25},{17,1},{25,9},{2,18},{10... | collective-permute-start | bytes 2752520 | tf_op jit(solution)/shard_map/ppermute | solution.py:43
  374.5 41.3 %collective-permute-start.7 = (f32[128,1792]{1,0:T(8,128)S(1)}, f32[128,1792]{1,0:T(8,128)S(1)}, u32[]{:S(2)}, u32[]{:S(2)}) collective-permute-start(f32[128,1792]{1,0:T(8,128)S(1)} %select_add_fusion.7), channel_id=1, source_target_pairs={{0,16},{8,24},{16,0},{24,8},{1,17},{9,25},{17,1},{25,9},{2,18},{10... | collective-permute-start | bytes 2752520 | tf_op jit(solution)/shard_map/ppermute | solution.py:43
  382.6 52.9 %collective-permute-start.37 = (f32[128,1792]{1,0:T(8,128)S(1)}, f32[128,1792]{1,0:T(8,128)S(1)}, u32[]{:S(2)}, u32[]{:S(2)}) collective-permute-start(f32[128,1792]{1,0:T(8,128)S(1)} %select_add_fusion.5), channel_id=1, source_target_pairs={{0,16},{8,24},{16,0},{24,8},{1,17},{9,25},{17,1},{25,9},{2,18},{10... | collective-permute-start | bytes 2752520 | tf_op jit(solution)/shard_map/ppermute | solution.py:43
  388.5 66.6 %collective-permute-start.52 = (f32[128,1792]{1,0:T(8,128)S(1)}, f32[128,1792]{1,0:T(8,128)S(1)}, u32[]{:S(2)}, u32[]{:S(2)}) collective-permute-start(f32[128,1792]{1,0:T(8,128)S(1)} %select_add_fusion.4), channel_id=1, source_target_pairs={{0,16},{8,24},{16,0},{24,8},{1,17},{9,25},{17,1},{25,9},{2,18},{10... | collective-permute-start | bytes 2752520 | tf_op jit(solution)/shard_map/ppermute | solution.py:43
  395.4 79.5 %collective-permute-start.67 = (f32[128,1792]{1,0:T(8,128)}, f32[128,1792]{1,0:T(8,128)}, u32[]{:S(2)}, u32[]{:S(2)}) collective-permute-start(f32[128,1792]{1,0:T(8,128)} %select_add_fusion.3), channel_id=1, source_target_pairs={{0,16},{8,24},{16,0},{24,8},{1,17},{9,25},{17,1},{25,9},{2,18},{10... | collective-permute-start | bytes 2752520 | tf_op jit(solution)/shard_map/ppermute | solution.py:43
  402.2 92.3 %collective-permute-start.82 = (f32[128,1792]{1,0:T(8,128)S(1)}, f32[128,1792]{1,0:T(8,128)}, u32[]{:S(2)}, u32[]{:S(2)}) collective-permute-start(f32[128,1792]{1,0:T(8,128)S(1)} %select_add_fusion.2), channel_id=1, source_target_pairs={{0,16},{8,24},{16,0},{24,8},{1,17},{9,25},{17,1},{25,9},{2,18},{10... | collective-permute-start | bytes 2752520 | tf_op jit(solution)/shard_map/ppermute | solution.py:43
  415.8 98.4 %collective-permute-start.97 = (f32[128,1792]{1,0:T(8,128)}, f32[128,1792]{1,0:T(8,128)}, u32[]{:S(2)}, u32[]{:S(2)}) collective-permute-start(f32[128,1792]{1,0:T(8,128)} %select_add_fusion.1), channel_id=1, source_target_pairs={{0,16},{8,24},{16,0},{24,8},{1,17},{9,25},{17,1},{25,9},{2,18},{10... | collective-permute-start | bytes 2752520 | tf_op jit(solution)/shard_map/ppermute | solution.py:43
  435.5 97.9 %collective-permute-start.112 = (f32[128,1792]{1,0:T(8,128)}, f32[128,1792]{1,0:T(8,128)}, u32[]{:S(2)}, u32[]{:S(2)}) collective-permute-start(f32[128,1792]{1,0:T(8,128)} %select_add_fusion), channel_id=1, source_target_pairs={{0,16},{8,24},{16,0},{24,8},{1,17},{9,25},{17,1},{25,9},{2,18},{10... | collective-permute-start | bytes 2752520 | tf_op jit(solution)/shard_map/ppermute | solution.py:43
  455.1 85.2 %collective-permute-start.23 = (f32[128,1792]{1,0:T(8,128)}, f32[128,1792]{1,0:T(8,128)}, u32[]{:S(2)}, u32[]{:S(2)}) collective-permute-start(f32[128,1792]{1,0:T(8,128)} %add.351), channel_id=1, source_target_pairs={{0,8},{8,0},{16,24},{24,16},{1,9},{9,1},{17,25},{25,17},{2,10},{10... | collective-permute-start | bytes 2752520 | tf_op jit(solution)/shard_map/ppermute | solution.py:45
  474.9 79.8 %collective-permute-start.8 = (f32[128,1792]{1,0:T(8,128)S(1)}, f32[128,1792]{1,0:T(8,128)S(1)}, u32[]{:S(2)}, u32[]{:S(2)}) collective-permute-start(f32[128,1792]{1,0:T(8,128)S(1)} %add.338), channel_id=1, source_target_pairs={{0,8},{8,0},{16,24},{24,16},{1,9},{9,1},{17,25},{25,17},{2,10},{10... | collective-permute-start | bytes 2752520 | tf_op jit(solution)/shard_map/ppermute | solution.py:45
  494.5 69.2 %collective-permute-start.38 = (f32[128,1792]{1,0:T(8,128)}, f32[128,1792]{1,0:T(8,128)}, u32[]{:S(2)}, u32[]{:S(2)}) collective-permute-start(f32[128,1792]{1,0:T(8,128)} %add.364), channel_id=1, source_target_pairs={{0,8},{8,0},{16,24},{24,16},{1,9},{9,1},{17,25},{25,17},{2,10},{10... | collective-permute-start | bytes 2752520 | tf_op jit(solution)/shard_map/ppermute | solution.py:45
  514.2 61.1 %collective-permute-start.53 = (f32[128,1792]{1,0:T(8,128)S(1)}, f32[128,1792]{1,0:T(8,128)}, u32[]{:S(2)}, u32[]{:S(2)}) collective-permute-start(f32[128,1792]{1,0:T(8,128)S(1)} %add.377), channel_id=1, source_target_pairs={{0,8},{8,0},{16,24},{24,16},{1,9},{9,1},{17,25},{25,17},{2,10},{10... | collective-permute-start | bytes 2752520 | tf_op jit(solution)/shard_map/ppermute | solution.py:45
  533.4 54.5 %collective-permute-start.68 = (f32[128,1792]{1,0:T(8,128)S(1)}, f32[128,1792]{1,0:T(8,128)}, u32[]{:S(2)}, u32[]{:S(2)}) collective-permute-start(f32[128,1792]{1,0:T(8,128)S(1)} %add.390), channel_id=1, source_target_pairs={{0,8},{8,0},{16,24},{24,16},{1,9},{9,1},{17,25},{25,17},{2,10},{10... | collective-permute-start | bytes 2752520 | tf_op jit(solution)/shard_map/ppermute | solution.py:45
  540.3 59.2 %collective-permute-start.83 = (f32[128,1792]{1,0:T(8,128)S(1)}, f32[128,1792]{1,0:T(8,128)}, u32[]{:S(2)}, u32[]{:S(2)}) collective-permute-start(f32[128,1792]{1,0:T(8,128)S(1)} %add.403), channel_id=1, source_target_pairs={{0,8},{8,0},{16,24},{24,16},{1,9},{9,1},{17,25},{25,17},{2,10},{10... | collective-permute-start | bytes 2752520 | tf_op jit(solution)/shard_map/ppermute | solution.py:45
  555.6 53.8 %collective-permute-start.98 = (f32[128,1792]{1,0:T(8,128)}, f32[128,1792]{1,0:T(8,128)}, u32[]{:S(2)}, u32[]{:S(2)}) collective-permute-start(f32[128,1792]{1,0:T(8,128)} %add.416), channel_id=1, source_target_pairs={{0,8},{8,0},{16,24},{24,16},{1,9},{9,1},{17,25},{25,17},{2,10},{10... | collective-permute-start | bytes 2752520 | tf_op jit(solution)/shard_map/ppermute | solution.py:45
  563.8 58.3 %collective-permute-start.113 = (f32[128,1792]{1,0:T(8,128)}, f32[128,1792]{1,0:T(8,128)}, u32[]{:S(2)}, u32[]{:S(2)}) collective-permute-start(f32[128,1792]{1,0:T(8,128)} %add.429), channel_id=1, source_target_pairs={{0,8},{8,0},{16,24},{24,16},{1,9},{9,1},{17,25},{25,17},{2,10},{10... | collective-permute-start | bytes 2752520 | tf_op jit(solution)/shard_map/ppermute | solution.py:45
  575.3 57.7 %collective-permute-start.24 = (f32[64,1792]{1,0:T(8,128)}, f32[64,1792]{1,0:T(8,128)}, u32[]{:S(2)}, u32[]{:S(2)}) collective-permute-start(f32[64,1792]{1,0:T(8,128)} %get-tuple-element.63), channel_id=1, source_target_pairs={{0,2},{1,3},{8,10},{9,11},{16,18},{17,19},{24,26},{25,27}} | collective-permute-start | bytes 1376264 | tf_op jit(solution)/shard_map/ppermute | solution.py:61
  587.9 46.0 %collective-permute-start.27 = (f32[64,1792]{1,0:T(8,128)}, f32[64,1792]{1,0:T(8,128)}, u32[]{:S(2)}, u32[]{:S(2)}) collective-permute-start(f32[64,1792]{1,0:T(8,128)} %get-tuple-element.64), channel_id=1, source_target_pairs={{6,4},{7,5},{14,12},{15,13},{22,20},{23,21},{30,28},{31,29}} | collective-permute-start | bytes 1376264 | tf_op jit(solution)/shard_map/ppermute | solution.py:62
  599.5 37.2 %collective-permute-start.12 = (f32[64,1792]{1,0:T(8,128)}, f32[64,1792]{1,0:T(8,128)}, u32[]{:S(2)}, u32[]{:S(2)}) collective-permute-start(f32[64,1792]{1,0:T(8,128)} %get-tuple-element.70), channel_id=1, source_target_pairs={{6,4},{7,5},{14,12},{15,13},{22,20},{23,21},{30,28},{31,29}} | collective-permute-start | bytes 1376264 | tf_op jit(solution)/shard_map/ppermute | solution.py:62
  676.0 29.5 %collective-permute-start.10 = (f32[64,1792]{1,0:T(8,128)S(1)}, f32[64,1792]{1,0:T(8,128)S(1)}, u32[]{:S(2)}, u32[]{:S(2)}) collective-permute-start(f32[64,1792]{1,0:T(8,128)S(1)} %get-tuple-element.67), channel_id=1, source_target_pairs={{0,2},{2,4},{1,3},{3,5},{8,10},{10,12},{9,11},{11,13},{16,18},{18,... | collective-permute-start | bytes 1376264 | tf_op jit(solution)/shard_map/ppermute | solution.py:61
  696.4 28.8 %collective-permute-start.55 = (f32[64,1792]{1,0:T(8,128)S(1)}, f32[64,1792]{1,0:T(8,128)S(1)}, u32[]{:S(2)}, u32[]{:S(2)}) collective-permute-start(f32[64,1792]{1,0:T(8,128)S(1)} %get-tuple-element.49), channel_id=1, source_target_pairs={{0,2},{2,4},{1,3},{3,5},{8,10},{10,12},{9,11},{11,13},{16,18},{18,... | collective-permute-start | bytes 1376264 | tf_op jit(solution)/shard_map/ppermute | solution.py:61
  716.0 28.8 %collective-permute-start.85 = (f32[64,1792]{1,0:T(8,128)S(1)}, f32[64,1792]{1,0:T(8,128)S(1)}, u32[]{:S(2)}, u32[]{:S(2)}) collective-permute-start(f32[64,1792]{1,0:T(8,128)S(1)} %get-tuple-element.37), channel_id=1, source_target_pairs={{0,2},{2,4},{1,3},{3,5},{8,10},{10,12},{9,11},{11,13},{16,18},{18,... | collective-permute-start | bytes 1376264 | tf_op jit(solution)/shard_map/ppermute | solution.py:61
  745.5 45.1 %collective-permute-start.26 = (f32[64,1792]{1,0:T(8,128)S(1)}, f32[64,1792]{1,0:T(8,128)S(1)}, u32[]{:S(2)}, u32[]{:S(2)}) collective-permute-start(f32[64,1792]{1,0:T(8,128)S(1)} %get-tuple-element.59), channel_id=1, source_target_pairs={{0,2},{2,4},{4,6},{1,3},{3,5},{5,7},{8,10},{10,12},{12,14},{9,11},... | collective-permute-start | bytes 1376264 | tf_op jit(solution)/shard_map/ppermute | solution.py:61
  754.6 37.3 %collective-permute-start.29 = (f32[64,1792]{1,0:T(8,128)S(1)}, f32[64,1792]{1,0:T(8,128)S(1)}, u32[]{:S(2)}, u32[]{:S(2)}) collective-permute-start(f32[64,1792]{1,0:T(8,128)S(1)} %get-tuple-element.60), channel_id=1, source_target_pairs={{6,4},{4,2},{2,0},{7,5},{5,3},{3,1},{14,12},{12,10},{10,8},{15,13}... | collective-permute-start | bytes 1376264 | tf_op jit(solution)/shard_map/ppermute | solution.py:62
  765.8 36.9 %collective-permute-start.41 = (f32[64,1792]{1,0:T(8,128)S(1)}, f32[64,1792]{1,0:T(8,128)S(1)}, u32[]{:S(2)}, u32[]{:S(2)}) collective-permute-start(f32[64,1792]{1,0:T(8,128)S(1)} %get-tuple-element.53), channel_id=1, source_target_pairs={{0,2},{2,4},{4,6},{1,3},{3,5},{5,7},{8,10},{10,12},{12,14},{9,11},... | collective-permute-start | bytes 1376264 | tf_op jit(solution)/shard_map/ppermute | solution.py:61
  (157 other events, 3743.9 us)

commit v2 on v0

v2 whole, which is shorter than its diff:
```python
import functools

import jax
import jax.numpy as jnp
from jax import lax
from jax.experimental import pallas as pl
from jax.experimental.pallas import tpu as pltpu
from jax.sharding import PartitionSpec as P

PERIOD = 896
SLAB = 512
CHUNK = 64
STRIP = 16
MESH = pl.DeviceIdType.MESH


def column_of(offset):
    return offset // SLAB * PERIOD + offset % SLAB


def tile_of(size):
    return 256 if size % 256 == 0 else 128 if size % 128 == 0 else size


def split(value):
    hi = value.astype(jnp.bfloat16)
    return hi, (value - hi.astype(jnp.float32)).astype(jnp.bfloat16)


def product3(hi, lo, other, contract):
    b_hi, b_lo = split(other)
    dot = functools.partial(
        lax.dot_general,
        dimension_numbers=(contract, ((), ())),
        preferred_element_type=jnp.float32,
    )
    return dot(hi, b_hi) + (dot(lo, b_hi) + dot(hi, b_lo))


def strips(rows, body):
    def step(i, carry):
        body(pl.multiple_of(i * STRIP, STRIP))
        return carry

    lax.fori_loop(0, rows // STRIP, step, 0)


def kernel(
    dims, w, a_hbm, x_hbm, out, a, x, ag, hi, lo, prod, core_in, bit_in, core_back, part, rs,
    keep, give, load_sem, own_sem, ag_send, ag_recv, core_send, core_recv, bit_send, bit_recv,
    back_send, back_recv, rs_send, rs_recv, give_send, give_recv, keep_sem,
):
    row_count, z, chunk, chunks, ring, rs_ring = dims
    row, col, depth = (lax.axis_index(n) for n in ("row", "col", "depth"))
    core = row % 2
    bits = [b for b in (2, 4, 8, 16, 32) if b < row_count]
    half = chunk * chunks
    group = z * chunk
    share = group // 2
    k_size, i_size = a.shape
    r_half = x.shape[0] // 2

    def partner(bit):
        return {"row": row + bit - 2 * bit * ((row // bit) % 2)}

    places = (col, z - 1 - col)
    targets = ({"col": col + 1}, {"col": col - 1})

    load_a = pltpu.make_async_copy(a_hbm, a, load_sem.at[0])
    load_x = pltpu.make_async_copy(x_hbm, x, load_sem.at[1])
    load_a.start()
    load_x.start()

    barrier = pltpu.get_barrier_semaphore()
    fixed = [partner(b) for b in [1] + bits] + [{"depth": 1 - depth}]
    for who in fixed:
        pl.semaphore_signal(barrier, inc=1, device_id=who, device_id_type=MESH)
    for way in range(2):

        @pl.when(places[way] < z - 1)
        def _():
            pl.semaphore_signal(barrier, inc=1, device_id=targets[way], device_id_type=MESH)

    ends = jnp.where(col == 0, 1, 0) + jnp.where(col == z - 1, 1, 0)
    pl.semaphore_wait(barrier, len(fixed) + 2 - ends)

    def remote(src, dst, send, recv, who):
        return pltpu.make_async_remote_copy(
            src_ref=src, dst_ref=dst, send_sem=send, recv_sem=recv,
            device_id=who, device_id_type=MESH,
        )

    def own_copy(c):
        return pltpu.make_async_copy(
            w.at[pl.ds(c * chunk, chunk)], ag.at[c % ring, 0], own_sem.at[c % ring]
        )

    def ag_copy(way, s, c):
        slot = c % ring
        came, lands = (z - s, z - 1 - s) if way == 0 else (s, s + 1)
        src = w.at[pl.ds(c * chunk, chunk)] if s == 0 else ag.at[slot, came]
        return remote(
            src, ag.at[slot, lands], ag_send.at[way, s, slot], ag_recv.at[way, s, slot],
            targets[way],
        )

    def rs_copy(way, s, c):
        slot = c % rs_ring
        src = part.at[c % z, z - 1 if way == 0 else 1] if s == 0 else rs.at[slot, way, s - 1]
        return remote(
            src, rs.at[slot, way, s], rs_send.at[way, s, slot], rs_recv.at[way, s, slot],
            targets[way],
        )

    mine = pl.ds(pl.multiple_of(core * share, share), share)
    theirs = pl.ds(pl.multiple_of((1 - core) * share, share), share)

    def core_copy(c):
        p = c % 2
        return remote(
            prod.at[p, theirs], core_in.at[p], core_send.at[p], core_recv.at[p], partner(1)
        )

    def back_copy(c):
        p = c % 2
        return remote(
            prod.at[p, mine], core_back.at[p], back_send.at[p], back_recv.at[p], partner(1)
        )

    def bit_copy(n, c):
        p = c % 2
        return remote(
            prod.at[p, mine], bit_in.at[n, p], bit_send.at[n, p], bit_recv.at[n, p],
            partner(bits[n]),
        )

    def give_copy(c):
        return remote(
            give.at[c % 2], out.at[pl.ds(depth * half + c * chunk, chunk)],
            give_send.at[c], give_recv.at[c], {"depth": 1 - depth},
        )

    def keep_copy(c):
        return pltpu.make_async_copy(
            keep.at[c % 2], out.at[pl.ds(depth * half + c * chunk, chunk)], keep_sem.at[c]
        )

    def live(c):
        return (c >= 0) & (c < chunks)

    def add_into_kept(p, other):
        base = core * share

        def body(r):
            at = pl.ds(pl.multiple_of(base + r, STRIP), STRIP)
            prod[p, at] = prod[p, at] + other[pl.ds(r, STRIP)]

        strips(share, body)

    def step(t, carry):
        for s in range(z - 1):
            c = t - 1 - s
            for way in range(2):
                place = places[way]

                @pl.when(live(c) & (place >= s + 1))
                def _():
                    ag_copy(way, s, c).wait_recv()

                @pl.when(live(c) & (place >= s) & (place < z - 1))
                def _():
                    ag_copy(way, s, c).wait_send()

        @pl.when(live(t - 1))
        def _():
            own_copy(t - 1).wait()

        for s in range(z - 1):
            c = t - 1 - z - s
            for way in range(2):
                place = places[way]

                @pl.when(live(c) & (place >= 1) & (place <= s + 1))
                def _():
                    rs_copy(way, s, c).wait_recv()

                @pl.when(live(c) & (place <= s) & (place < z - 1))
                def _():
                    rs_copy(way, s, c).wait_send()

        for s in range(z - 1):
            c = t - s
            for way in range(2):

                @pl.when(live(c) & (places[way] >= s) & (places[way] < z - 1))
                def _():
                    ag_copy(way, s, c).start()

        @pl.when(live(t))
        def _():
            own_copy(t).start()

        for s in range(1, z - 1):
            c = t - z - s
            for way in range(2):
                place = places[way]
                slot = c % rs_ring
                term = part.at[c % z, z - 1 - s if way == 0 else s + 1]
                sum_ref = rs.at[slot, way, s - 1]

                @pl.when(live(c) & (place >= 1) & (place <= s) & (place < z - 1))
                def _():
                    def body(r):
                        at = pl.ds(r, STRIP)
                        sum_ref[at] = sum_ref[at] + term[at]

                    strips(chunk, body)

                @pl.when(live(c) & (place == 0))
                def _():
                    def body(r):
                        at = pl.ds(r, STRIP)
                        sum_ref[at] = term[at]

                    strips(chunk, body)

                @pl.when(live(c) & (place <= s) & (place < z - 1))
                def _():
                    rs_copy(way, s, c).start()

        last = t - (2 * z - 1)

        @pl.when(live(last))
        def _():
            total = part.at[last % z, 0]
            for way in range(2):

                @pl.when(places[way] > 0)
                def _():
                    def body(r):
                        at = pl.ds(r, STRIP)
                        total[at] = total[at] + rs[last % rs_ring, way, z - 2, at]

                    strips(chunk, body)

            @pl.when(last >= 2)
            def _():
                give_copy(last - 2).wait_send()
                keep_copy(last - 2).wait()

            def halve(first, second):
                def body(r):
                    at = pl.ds(r, STRIP)
                    value = total[at]
                    first[last % 2, at] = value[:, :r_half]
                    second[last % 2, at] = value[:, r_half:]

                strips(chunk, body)

            @pl.when(depth == 0)
            def _():
                halve(keep, give)

            @pl.when(depth == 1)
            def _():
                halve(give, keep)

            give_copy(last).start()
            keep_copy(last).start()

        c2 = t - z
        p2 = c2 % 2

        @pl.when(live(c2))
        def _():
            for n in range(len(bits)):
                if n > 0:
                    bit_copy(n, c2).start()
                bit_copy(n, c2).wait()
                add_into_kept(p2, bit_in.at[n, p2])
            back_copy(c2).start()

        c1 = t - (z - 1)
        p1 = c1 % 2

        @pl.when(live(c1))
        def _():
            @pl.when(c1 == 0)
            def _():
                load_a.wait()

            for slot in range(z):

                def body(r):
                    h, l = split(ag[c1 % ring, slot, pl.ds(r, STRIP)])
                    at = pl.ds(pl.multiple_of(slot * chunk + r, STRIP), STRIP)
                    hi[at, :k_size] = h
                    lo[at, :k_size] = l

                strips(chunk, body)
            tile = tile_of(i_size)

            def body(j, carry):
                cols = pl.ds(pl.multiple_of(j * tile, tile), tile)
                prod[p1, :, cols] = product3(
                    hi[:, :k_size], lo[:, :k_size], a[:, cols], ((1,), (0,))
                )
                return carry

            lax.fori_loop(0, i_size // tile, body, 0)
            core_copy(c1).start()

        @pl.when(live(c2))
        def _():
            @pl.when(c2 == 0)
            def _():
                load_x.wait()

            back_copy(c2).wait()
            offset = depth * half + c2 * chunk
            here = offset // SLAB * PERIOD + offset % SLAB

            def residual(base, source):
                def body(r):
                    at = pl.multiple_of(base + r, STRIP)
                    value = source(r, at)
                    line = lax.broadcasted_iota(jnp.int32, value.shape, 0) + at
                    place = lax.broadcasted_iota(jnp.int32, value.shape, 1)
                    select = (line < chunk) & (place == here + line)
                    h, l = split(jnp.where(select, 2.0, 0.0) - value)
                    hi[pl.ds(at, STRIP), :i_size] = h
                    lo[pl.ds(at, STRIP), :i_size] = l

                strips(share, body)

            residual(core * share, lambda r, at: prod[p2, pl.ds(at, STRIP)])
            residual((1 - core) * share, lambda r, at: core_back[p2, pl.ds(r, STRIP)])
            tile = tile_of(x.shape[0])

            def body(j, carry):
                lines = pl.ds(pl.multiple_of(j * tile, tile), tile)
                value = product3(hi[:, :i_size], lo[:, :i_size], x[lines], ((1,), (1,)))
                part[c2 % z, :, :, lines] = value.reshape(z, chunk, tile)
                return carry

            lax.fori_loop(0, x.shape[0] // tile, body, 0)
            for way in range(2):

                @pl.when(places[way] == 0)
                def _():
                    rs_copy(way, 0, c2).start()

        @pl.when(live(c1))
        def _():
            core_copy(c1).wait()
            add_into_kept(p1, core_in.at[p1])
            bit_copy(0, c1).start()

        return carry

    lax.fori_loop(0, chunks + 2 * z - 1, step, 0)
    for c in range(chunks):
        give_copy(c).wait_recv()
        if c >= chunks - 2:
            give_copy(c).wait_send()
            keep_copy(c).wait()


def refresh(dims, w, covariance, iterate):
    row_count, z, chunk, chunks, ring, rs_ring = dims
    k_size, i_size = covariance.shape
    r_size = iterate.shape[0]
    n_bits = max(1, row_count.bit_length() - 2)
    group = z * chunk
    share = group // 2
    f32, bf16, dma = jnp.float32, jnp.bfloat16, pltpu.SemaphoreType.DMA
    anywhere = pl.BlockSpec(memory_space=pl.ANY)
    flops = 2 * 3 * 2 * group * chunks * k_size * i_size
    return pl.pallas_call(
        functools.partial(kernel, dims),
        out_shape=jax.ShapeDtypeStruct((2 * chunk * chunks, r_size // 2), f32),
        in_specs=[anywhere] * 3,
        out_specs=anywhere,
        scratch_shapes=[
            pltpu.VMEM((k_size, i_size), f32),
            pltpu.VMEM((r_size, i_size), f32),
            pltpu.VMEM((ring, z, chunk, k_size), f32),
            pltpu.VMEM((group, i_size if i_size >= k_size else k_size), bf16),
            pltpu.VMEM((group, i_size if i_size >= k_size else k_size), bf16),
            pltpu.VMEM((2, group, i_size), f32),
            pltpu.VMEM((2, share, i_size), f32),
            pltpu.VMEM((n_bits, 2, share, i_size), f32),
            pltpu.VMEM((2, share, i_size), f32),
            pltpu.VMEM((z, z, chunk, r_size), f32),
            pltpu.VMEM((rs_ring, 2, z - 1, chunk, r_size), f32),
            pltpu.VMEM((2, chunk, r_size // 2), f32),
            pltpu.VMEM((2, chunk, r_size // 2), f32),
            dma((2,)),
            dma((ring,)),
            dma((2, z - 1, ring)),
            dma((2, z - 1, ring)),
            dma((2,)),
            dma((2,)),
            dma((n_bits, 2)),
            dma((n_bits, 2)),
            dma((2,)),
            dma((2,)),
            dma((2, z - 1, rs_ring)),
            dma((2, z - 1, rs_ring)),
            dma((chunks,)),
            dma((chunks,)),
            dma((chunks,)),
        ],
        compiler_params=pltpu.CompilerParams(
            collective_id=0, has_side_effects=True, vmem_limit_bytes=VMEM_LIMIT
        ),
        cost_estimate=pl.CostEstimate(flops=flops, bytes_accessed=40000000, transcendentals=0),
    )(w, covariance, iterate)


VMEM_LIMIT = 65000000


def solution(mesh):
    row_count, z = mesh.shape["row"], mesh.shape["col"]

    def local(covariance, iterate):
        half = covariance.shape[1] // PERIOD * SLAB // 2
        chunk = min(CHUNK, half)
        chunks = half // chunk
        dims = (row_count, z, chunk, chunks, min(chunks, z + 1), min(chunks, z - 1))
        piece = min(half, SLAB)
        depth = lax.axis_index("depth")
        window = []
        for start in range(0, half, piece):
            near, far = column_of(start), column_of(half + start)
            window.append(
                jnp.where(
                    depth == 0,
                    iterate[:, near : near + piece],
                    iterate[:, far : far + piece],
                ).T
            )
        w = jnp.concatenate(window, axis=0)
        return refresh(dims, w, covariance, iterate).T

    in_specs = (P("row", "col"), P("row", "col"))
    out_specs = P(("row", "depth"), "col")
    return jax.shard_map(local, mesh=mesh, in_specs=in_specs, out_specs=out_specs, check_vma=False)
```

time: 1550 us -> 422 us (0.27)
  waiting for transfers between devices: 1270 us -> 0 us
  Pallas kernels: 0 us -> 395 us
  matrix products: 181 us -> 0 us
  local copies, waits for them, and re-layouts: 79.1 us -> 22.3 us
    all_gather x4 -> x0, waiting for transfers between devices: 1030 us -> none  [the longest x1 435 us: local(): lax.all_gather(cov_half, 'col', axis=1, tiled=True)]
    pallas_call x0 -> x1, Pallas kernels: none -> 395 us  [refresh(): pl.pallas_call(functools.partial(kernel, dims), out_shape=jax.ShapeDtypeS...]
    dot_general x2 -> x0, matrix products: 181 us -> none  [the longest x1 90.5 us: local(): jnp.dot(lax.all_gather(cov_half, 'col', axis=1, tiled=True), rows_part, p...]
    psum x1 -> x0, waiting for transfers between devices: 149 us -> none  [local(): full_product = lax.psum(partial_product, 'depth')]
    reduce_scatter x1 -> x0, waiting for transfers between devices: 88.6 us -> none  [local(): lax.psum_scatter(partial_result, 'depth', scatter_dimension=0, tiled=True)]
    reshape x3 -> x0, local copies, waits for them, and re-layouts: 46.7 us -> none  [the longest x2 31.1 us: contraction_half(): shaped = matrix.reshape(tile_rows, blocks, 2, half_rows)]
    dynamic_slice x3 -> x0, local copies, waits for them, and re-layouts: 24.6 us -> none  [the longest x2 20.2 us: contraction_half(): picked = lax.dynamic_index_in_dim(shaped, depth_pos, 2, keepdims=False)]
  transfers between devices with their start and end apart: 6 -> 0, of which waited for: 6 -> 0; matrix products, arithmetic and copies ran while one was open for 4% -> 0% of each run, Pallas kernels for 0% -> 0%
where the time goes in v2:
time: 422 us
  Pallas kernels  395 us (94%)
  local copies, waits for them, and re-layouts  22.3 us (5%)
  other arithmetic  4.32 us (1%)
    pallas_call x1, Pallas kernels, refresh(): pl.pallas_call(functools.partial(kernel, dims), out_shape=jax.ShapeDtypeS...  395 us
    unnamed x2, local copies, waits for them, and re-layouts  10.3 us

profile of v2, /device:TPU:0, one launch (start us, length us, event | category | flops | bytes accessed | tf_op | source)
XLA Modules:
  0.0 421.9 jit_solution(18139854862010565963)
XLA Ops:
  0.0 7.0 %fusion = (f32[1792,512]{1,0:T(8,128)}, f32[1792,512]{1,0:T(8,128)}) fusion(f32[1792,1792]{1,0:T(8,128)} %x_hbm.1), kind=kLoop, calls=%fused_computation.1 | loop fusion | bytes 14680064 | tf_op jit(solution)/shard_map/slice | solution.py:441
  7.0 5.1 %copy.6 = f32[1792,512]{0,1:T(8,128)} copy(f32[1792,512]{1,0:T(8,128)} %get-tuple-element.6) | data formatting | bytes 7340032
  12.2 5.1 %copy.7 = f32[1792,512]{0,1:T(8,128)} copy(f32[1792,512]{1,0:T(8,128)} %get-tuple-element.5) | data formatting | bytes 7340032
  17.3 4.3 %select_bitcast_fusion.w = f32[512,1792]{1,0:T(8,128)} fusion(f32[1792,512]{0,1:T(8,128)} %copy.6, f32[1792,512]{0,1:T(8,128)} %copy.7, pred[]{:T(512)S(6)} %eq.3), kind=kLoop, calls=%fused_computation | loop fusion | flops 917504 | bytes 11010049 | tf_op jit(solution)/shard_map/transpose | solution.py:442
  21.7 395.3 %shard_map.28 = f32[1024,896]{1,0:T(8,128)} custom-call(f32[512,1792]{1,0:T(8,128)} %select_bitcast_fusion.w, f32[1792,1792]{1,0:T(8,128)} %a_hbm.1, f32[1792,1792]{1,0:T(8,128)} %x_hbm.1), custom_call_target="tpu_custom_call" | custom-call | flops 78920024064 | bytes 40000000 | tf_op jit(solution)/shard_map/pallas_call | solution.py:379
  416.9 5.0 %copy.5 = f32[896,1024]{1,0:T(8,128)} copy(f32[896,1024]{0,1:T(8,128)} %bitcast.3) | data formatting | bytes 7340032 | tf_op jit(solution)/shard_map/transpose | solution.py:445

commit v3 on v2

--- a/solution.py
+++ b/solution.py
@@ -12,10 +12,6 @@
 CHUNK = 64
 STRIP = 16
 MESH = pl.DeviceIdType.MESH
-
-
-def column_of(offset):
-    return offset // SLAB * PERIOD + offset % SLAB
 
 
 def tile_of(size):
@@ -46,8 +42,8 @@
 
 
 def kernel(
-    dims, w, a_hbm, x_hbm, out, a, x, ag, hi, lo, prod, core_in, bit_in, core_back, part, rs,
-    keep, give, load_sem, own_sem, ag_send, ag_recv, core_send, core_recv, bit_send, bit_recv,
+    dims, a_hbm, x_hbm, out, a, x, ag, hi, lo, prod, core_in, bit_in, core_back, part, rs,
+    keep, give, load_sem, ag_send, ag_recv, core_send, core_recv, bit_send, bit_recv,
     back_send, back_recv, rs_send, rs_recv, give_send, give_recv, keep_sem,
 ):
     row_count, z, chunk, chunks, ring, rs_ring = dims
@@ -68,7 +64,6 @@
 
     load_a = pltpu.make_async_copy(a_hbm, a, load_sem.at[0])
     load_x = pltpu.make_async_copy(x_hbm, x, load_sem.at[1])
-    load_a.start()
     load_x.start()
 
     barrier = pltpu.get_barrier_semaphore()
@@ -90,17 +85,11 @@
             device_id=who, device_id_type=MESH,
         )
 
-    def own_copy(c):
-        return pltpu.make_async_copy(
-            w.at[pl.ds(c * chunk, chunk)], ag.at[c % ring, 0], own_sem.at[c % ring]
-        )
-
     def ag_copy(way, s, c):
         slot = c % ring
-        came, lands = (z - s, z - 1 - s) if way == 0 else (s, s + 1)
-        src = w.at[pl.ds(c * chunk, chunk)] if s == 0 else ag.at[slot, came]
-        return remote(
-            src, ag.at[slot, lands], ag_send.at[way, s, slot], ag_recv.at[way, s, slot],
+        came, lands = ((z - s) % z, z - 1 - s) if way == 0 else (s, s + 1)
+        return remote(
+            ag.at[slot, came], ag.at[slot, lands], ag_send.at[way, s, slot], ag_recv.at[way, s, slot],
             targets[way],
         )
 
@@ -157,6 +146,10 @@
 
         strips(share, body)
 
+    load_x.wait()
+    load_a.start()
+    pair = min(chunks, max(1, 128 // chunk))
+
     def step(t, carry):
         for s in range(z - 1):
             c = t - 1 - s
@@ -171,9 +164,63 @@
                 def _():
                     ag_copy(way, s, c).wait_send()
 
-        @pl.when(live(t - 1))
-        def _():
-            own_copy(t - 1).wait()
+        @pl.when((t % pair == 0) & (t < chunks))
+        def _():
+            offset = depth * half + t * chunk
+            here = offset // SLAB * PERIOD + offset % SLAB
+            block = x[:, pl.ds(pl.multiple_of(here, pair * chunk), pair * chunk)].T
+            for n in range(pair):
+                ag[(t + n) % ring, 0] = block[n * chunk : (n + 1) * chunk]
+
+        for s in reversed(range(z - 1)):
+            c = t - s
+            for way in range(2):
+
+                @pl.when(live(c) & (places[way] >= s) & (places[way] < z - 1))
+                def _():
+                    ag_copy(way, s, c).start()
+
+        c2 = t - z
+        p2 = c2 % 2
+
+        c1 = t - (z - 1)
+        p1 = c1 % 2
+
+        @pl.when(live(c1))
+        def _():
+            @pl.when(c1 == 0)
+            def _():
+                load_a.wait()
+
+            for slot in range(z):
+
+                def body(r):
+                    h, l = split(ag[c1 % ring, slot, pl.ds(r, STRIP)])
+                    at = pl.ds(pl.multiple_of(slot * chunk + r, STRIP), STRIP)
+                    hi[at, :k_size] = h
+                    lo[at, :k_size] = l
+
+                strips(chunk, body)
+            tile = tile_of(i_size)
+
+            def body(j, carry):
+                cols = pl.ds(pl.multiple_of(j * tile, tile), tile)
+                prod[p1, :, cols] = product3(
+                    hi[:, :k_size], lo[:, :k_size], a[:, cols], ((1,), (0,))
+                )
+                return carry
+
+            lax.fori_loop(0, i_size // tile, body, 0)
+            core_copy(c1).start()
+
+        @pl.when(live(c2))
+        def _():
+            for n in range(len(bits)):
+                if n > 0:
+                    bit_copy(n, c2).start()
+                bit_copy(n, c2).wait()
+                add_into_kept(p2, bit_in.at[n, p2])
+            back_copy(c2).start()
 
         for s in range(z - 1):
             c = t - 1 - z - s
@@ -187,18 +234,6 @@
                 @pl.when(live(c) & (place <= s) & (place < z - 1))
                 def _():
                     rs_copy(way, s, c).wait_send()
-
-        for s in range(z - 1):
-            c = t - s
-            for way in range(2):
-
-                @pl.when(live(c) & (places[way] >= s) & (places[way] < z - 1))
-                def _():
-                    ag_copy(way, s, c).start()
-
-        @pl.when(live(t))
-        def _():
-            own_copy(t).start()
 
         for s in range(1, z - 1):
             c = t - z - s
@@ -268,54 +303,8 @@
             give_copy(last).start()
             keep_copy(last).start()
 
-        c2 = t - z
-        p2 = c2 % 2
-
         @pl.when(live(c2))
         def _():
-            for n in range(len(bits)):
-                if n > 0:
-                    bit_copy(n, c2).start()
-                bit_copy(n, c2).wait()
-                add_into_kept(p2, bit_in.at[n, p2])
-            back_copy(c2).start()
-
-        c1 = t - (z - 1)
-        p1 = c1 % 2
-
-        @pl.when(live(c1))
-        def _():
-            @pl.when(c1 == 0)
-            def _():
-                load_a.wait()
-
-            for slot in range(z):
-
-                def body(r):
-                    h, l = split(ag[c1 % ring, slot, pl.ds(r, STRIP)])
-                    at = pl.ds(pl.multiple_of(slot * chunk + r, STRIP), STRIP)
-                    hi[at, :k_size] = h
-                    lo[at, :k_size] = l
-
-                strips(chunk, body)
-            tile = tile_of(i_size)
-
-            def body(j, carry):
-                cols = pl.ds(pl.multiple_of(j * tile, tile), tile)
-                prod[p1, :, cols] = product3(
-                    hi[:, :k_size], lo[:, :k_size], a[:, cols], ((1,), (0,))
-                )
-                return carry
-
-            lax.fori_loop(0, i_size // tile, body, 0)
-            core_copy(c1).start()
-
-        @pl.when(live(c2))
-        def _():
-            @pl.when(c2 == 0)
-            def _():
-                load_x.wait()
-
             back_copy(c2).wait()
             offset = depth * half + c2 * chunk
             here = offset // SLAB * PERIOD + offset % SLAB
@@ -335,6 +324,15 @@
 
             residual(core * share, lambda r, at: prod[p2, pl.ds(at, STRIP)])
             residual((1 - core) * share, lambda r, at: core_back[p2, pl.ds(r, STRIP)])
+
+        @pl.when(live(c1))
+        def _():
+            core_copy(c1).wait()
+            add_into_kept(p1, core_in.at[p1])
+            bit_copy(0, c1).start()
+
+        @pl.when(live(c2))
+        def _():
             tile = tile_of(x.shape[0])
 
             def body(j, carry):
@@ -349,12 +347,6 @@
                 @pl.when(places[way] == 0)
                 def _():
                     rs_copy(way, 0, c2).start()
-
-        @pl.when(live(c1))
-        def _():
-            core_copy(c1).wait()
-            add_into_kept(p1, core_in.at[p1])
-            bit_copy(0, c1).start()
 
         return carry
 
@@ -366,7 +358,7 @@
             keep_copy(c).wait()
 
 
-def refresh(dims, w, covariance, iterate):
+def refresh(dims, covariance, iterate):
     row_count, z, chunk, chunks, ring, rs_ring = dims
     k_size, i_size = covariance.shape
     r_size = iterate.shape[0]
@@ -379,7 +371,7 @@
     return pl.pallas_call(
         functools.partial(kernel, dims),
         out_shape=jax.ShapeDtypeStruct((2 * chunk * chunks, r_size // 2), f32),
-        in_specs=[anywhere] * 3,
+        in_specs=[anywhere] * 2,
         out_specs=anywhere,
         scratch_shapes=[
             pltpu.VMEM((k_size, i_size), f32),
@@ -396,7 +388,6 @@
             pltpu.VMEM((2, chunk, r_size // 2), f32),
             pltpu.VMEM((2, chunk, r_size // 2), f32),
             dma((2,)),
-            dma((ring,)),
             dma((2, z - 1, ring)),
             dma((2, z - 1, ring)),
             dma((2,)),
@@ -415,7 +406,7 @@
             collective_id=0, has_side_effects=True, vmem_limit_bytes=VMEM_LIMIT
         ),
         cost_estimate=pl.CostEstimate(flops=flops, bytes_accessed=40000000, transcendentals=0),
-    )(w, covariance, iterate)
+    )(covariance, iterate)
 
 
 VMEM_LIMIT = 65000000
@@ -429,20 +420,7 @@
         chunk = min(CHUNK, half)
         chunks = half // chunk
         dims = (row_count, z, chunk, chunks, min(chunks, z + 1), min(chunks, z - 1))
-        piece = min(half, SLAB)
-        depth = lax.axis_index("depth")
-        window = []
-        for start in range(0, half, piece):
-            near, far = column_of(start), column_of(half + start)
-            window.append(
-                jnp.where(
-                    depth == 0,
-                    iterate[:, near : near + piece],
-                    iterate[:, far : far + piece],
-                ).T
-            )
-        w = jnp.concatenate(window, axis=0)
-        return refresh(dims, w, covariance, iterate).T
+        return refresh(dims, covariance, iterate).T
 
     in_specs = (P("row", "col"), P("row", "col"))
     out_specs = P(("row", "depth"), "col")

time: 422 us -> 402 us (0.953)
  local copies, waits for them, and re-layouts: 22.3 us -> 4.99 us
  other arithmetic: 4.32 us -> 0 us
    unnamed x2 -> x0, local copies, waits for them, and re-layouts: 10.3 us -> none
    slice x1 -> x0, local copies, waits for them, and re-layouts: 7.05 us -> none  [local(): iterate[:, far:far + piece]]
    transpose x1 -> x0, other arithmetic: 4.32 us -> none  [local(): window.append(jnp.where(depth == 0, iterate[:, near:near + piece], iterat...]
where the time goes in v3:
time: 402 us
  Pallas kernels  397 us (99%)
  local copies, waits for them, and re-layouts  4.99 us (1%)
    pallas_call x1, Pallas kernels, refresh(): pl.pallas_call(functools.partial(kernel, dims), out_shape=jax.ShapeDtypeS...  397 us

profile of v3, /device:TPU:0, one launch (start us, length us, event | category | flops | bytes accessed | tf_op | source)
XLA Modules:
  0.0 401.7 jit_solution(1308670264560187683)
XLA Ops:
  0.0 396.7 %shard_map.28 = f32[1024,896]{1,0:T(8,128)} custom-call(f32[1792,1792]{1,0:T(8,128)} %a_hbm.1, f32[1792,1792]{1,0:T(8,128)} %x_hbm.1), custom_call_target="tpu_custom_call" | custom-call | flops 78920024064 | bytes 40000000 | tf_op jit(solution)/shard_map/pallas_call | solution.py:371
  396.7 5.0 %copy.3 = f32[896,1024]{1,0:T(8,128)} copy(f32[896,1024]{0,1:T(8,128)} %bitcast.1) | data formatting | bytes 7340032 | tf_op jit(solution)/shard_map/transpose | solution.py:423

commit v4 on v3

--- a/solution.py
+++ b/solution.py
@@ -23,14 +23,16 @@
     return hi, (value - hi.astype(jnp.float32)).astype(jnp.bfloat16)
 
 
-def product3(hi, lo, other, contract):
+def product3(both, other, contract):
     b_hi, b_lo = split(other)
     dot = functools.partial(
         lax.dot_general,
         dimension_numbers=(contract, ((), ())),
         preferred_element_type=jnp.float32,
     )
-    return dot(hi, b_hi) + (dot(lo, b_hi) + dot(hi, b_lo))
+    rows = both.shape[0] // 2
+    first = dot(both, b_hi)
+    return first[:rows] + (first[rows:] + dot(both[:rows], b_lo))
 
 
 def strips(rows, body):
@@ -42,7 +44,7 @@
 
 
 def kernel(
-    dims, a_hbm, x_hbm, out, a, x, ag, hi, lo, prod, core_in, bit_in, core_back, part, rs,
+    dims, a_hbm, x_hbm, out, a, x, ag, both, prod, core_in, bit_in, core_back, part, rs,
     keep, give, load_sem, ag_send, ag_recv, core_send, core_recv, bit_send, bit_recv,
     back_send, back_recv, rs_send, rs_recv, give_send, give_recv, keep_sem,
 ):
@@ -150,20 +152,78 @@
     load_a.start()
     pair = min(chunks, max(1, 128 // chunk))
 
+    def transfers(t, e):
+        for s in range(z - 1):
+            if (e - 1 - s) % 2:
+                continue
+            c = t + (e - 1 - s) // 2
+            for way in range(2):
+                place = places[way]
+
+                @pl.when(live(c) & (place >= s + 1))
+                def _():
+                    ag_copy(way, s, c).wait_recv()
+
+                @pl.when(live(c) & (place >= s) & (place < z - 1))
+                def _():
+                    ag_copy(way, s, c).wait_send()
+
+        for s in reversed(range(z - 1)):
+            if (e - s) % 2:
+                continue
+            c = t + (e - s) // 2
+            for way in range(2):
+
+                @pl.when(live(c) & (places[way] >= s) & (places[way] < z - 1))
+                def _():
+                    ag_copy(way, s, c).start()
+
+        for s in range(z - 1):
+            if (e - z - 4 - s) % 2:
+                continue
+            c = t + (e - z - 4 - s) // 2
+            for way in range(2):
+                place = places[way]
+
+                @pl.when(live(c) & (place >= 1) & (place <= s + 1))
+                def _():
+                    rs_copy(way, s, c).wait_recv()
+
+                @pl.when(live(c) & (place <= s) & (place < z - 1))
+                def _():
+                    rs_copy(way, s, c).wait_send()
+
+        for s in range(1, z - 1):
+            if (e - z - 3 - s) % 2:
+                continue
+            c = t + (e - z - 3 - s) // 2
+            for way in range(2):
+                place = places[way]
+                slot = c % rs_ring
+                term = part.at[c % z, z - 1 - s if way == 0 else s + 1]
+                sum_ref = rs.at[slot, way, s - 1]
+
+                @pl.when(live(c) & (place >= 1) & (place <= s) & (place < z - 1))
+                def _():
+                    def body(r):
+                        at = pl.ds(r, STRIP)
+                        sum_ref[at] = sum_ref[at] + term[at]
+
+                    strips(chunk, body)
+
+                @pl.when(live(c) & (place == 0))
+                def _():
+                    def body(r):
+                        at = pl.ds(r, STRIP)
+                        sum_ref[at] = term[at]
+
+                    strips(chunk, body)
+
+                @pl.when(live(c) & (place <= s) & (place < z - 1))
+                def _():
+                    rs_copy(way, s, c).start()
+
     def step(t, carry):
-        for s in range(z - 1):
-            c = t - 1 - s
-            for way in range(2):
-                place = places[way]
-
-                @pl.when(live(c) & (place >= s + 1))
-                def _():
-                    ag_copy(way, s, c).wait_recv()
-
-                @pl.when(live(c) & (place >= s) & (place < z - 1))
-                def _():
-                    ag_copy(way, s, c).wait_send()
-
         @pl.when((t % pair == 0) & (t < chunks))
         def _():
             offset = depth * half + t * chunk
@@ -172,98 +232,9 @@
             for n in range(pair):
                 ag[(t + n) % ring, 0] = block[n * chunk : (n + 1) * chunk]
 
-        for s in reversed(range(z - 1)):
-            c = t - s
-            for way in range(2):
-
-                @pl.when(live(c) & (places[way] >= s) & (places[way] < z - 1))
-                def _():
-                    ag_copy(way, s, c).start()
-
-        c2 = t - z
-        p2 = c2 % 2
-
-        c1 = t - (z - 1)
-        p1 = c1 % 2
-
-        @pl.when(live(c1))
-        def _():
-            @pl.when(c1 == 0)
-            def _():
-                load_a.wait()
-
-            for slot in range(z):
-
-                def body(r):
-                    h, l = split(ag[c1 % ring, slot, pl.ds(r, STRIP)])
-                    at = pl.ds(pl.multiple_of(slot * chunk + r, STRIP), STRIP)
-                    hi[at, :k_size] = h
-                    lo[at, :k_size] = l
-
-                strips(chunk, body)
-            tile = tile_of(i_size)
-
-            def body(j, carry):
-                cols = pl.ds(pl.multiple_of(j * tile, tile), tile)
-                prod[p1, :, cols] = product3(
-                    hi[:, :k_size], lo[:, :k_size], a[:, cols], ((1,), (0,))
-                )
-                return carry
-
-            lax.fori_loop(0, i_size // tile, body, 0)
-            core_copy(c1).start()
-
-        @pl.when(live(c2))
-        def _():
-            for n in range(len(bits)):
-                if n > 0:
-                    bit_copy(n, c2).start()
-                bit_copy(n, c2).wait()
-                add_into_kept(p2, bit_in.at[n, p2])
-            back_copy(c2).start()
-
-        for s in range(z - 1):
-            c = t - 1 - z - s
-            for way in range(2):
-                place = places[way]
-
-                @pl.when(live(c) & (place >= 1) & (place <= s + 1))
-                def _():
-                    rs_copy(way, s, c).wait_recv()
-
-                @pl.when(live(c) & (place <= s) & (place < z - 1))
-                def _():
-                    rs_copy(way, s, c).wait_send()
-
-        for s in range(1, z - 1):
-            c = t - z - s
-            for way in range(2):
-                place = places[way]
-                slot = c % rs_ring
-                term = part.at[c % z, z - 1 - s if way == 0 else s + 1]
-                sum_ref = rs.at[slot, way, s - 1]
-
-                @pl.when(live(c) & (place >= 1) & (place <= s) & (place < z - 1))
-                def _():
-                    def body(r):
-                        at = pl.ds(r, STRIP)
-                        sum_ref[at] = sum_ref[at] + term[at]
-
-                    strips(chunk, body)
-
-                @pl.when(live(c) & (place == 0))
-                def _():
-                    def body(r):
-                        at = pl.ds(r, STRIP)
-                        sum_ref[at] = term[at]
-
-                    strips(chunk, body)
-
-                @pl.when(live(c) & (place <= s) & (place < z - 1))
-                def _():
-                    rs_copy(way, s, c).start()
-
-        last = t - (2 * z - 1)
+        transfers(t, 0)
+
+        last = t - z - 1
 
         @pl.when(live(last))
         def _():
@@ -302,6 +273,9 @@
 
             give_copy(last).start()
             keep_copy(last).start()
+
+        c2 = t - z // 2 - 1
+        p2 = c2 % 2
 
         @pl.when(live(c2))
         def _():
@@ -317,13 +291,74 @@
                     place = lax.broadcasted_iota(jnp.int32, value.shape, 1)
                     select = (line < chunk) & (place == here + line)
                     h, l = split(jnp.where(select, 2.0, 0.0) - value)
-                    hi[pl.ds(at, STRIP), :i_size] = h
-                    lo[pl.ds(at, STRIP), :i_size] = l
+                    both[pl.ds(at, STRIP), :i_size] = h
+                    both[pl.ds(pl.multiple_of(group + at, STRIP), STRIP), :i_size] = l
 
                 strips(share, body)
 
             residual(core * share, lambda r, at: prod[p2, pl.ds(at, STRIP)])
             residual((1 - core) * share, lambda r, at: core_back[p2, pl.ds(r, STRIP)])
+
+
+        @pl.when(live(c2))
+        def _():
+            tile = tile_of(x.shape[0])
+
+            def body(j, carry):
+                lines = pl.ds(pl.multiple_of(j * tile, tile), tile)
+                value = product3(both[:, :i_size], x[lines], ((1,), (1,)))
+                part[c2 % z, :, :, lines] = value.reshape(z, chunk, tile)
+                return carry
+
+            lax.fori_loop(0, x.shape[0] // tile, body, 0)
+            for way in range(2):
+
+                @pl.when(places[way] == 0)
+                def _():
+                    rs_copy(way, 0, c2).start()
+
+        transfers(t, 1)
+        c1 = t - z // 2 + 1
+        p1 = c1 % 2
+
+        @pl.when(live(c1))
+        def _():
+            @pl.when(c1 == 0)
+            def _():
+                load_a.wait()
+
+            for slot in range(z):
+
+                def body(r):
+                    h, l = split(ag[c1 % ring, slot, pl.ds(r, STRIP)])
+                    at = pl.ds(pl.multiple_of(slot * chunk + r, STRIP), STRIP)
+                    both[at, :k_size] = h
+                    both[pl.ds(pl.multiple_of(group + slot * chunk + r, STRIP), STRIP), :k_size] = l
+
+                strips(chunk, body)
+            tile = tile_of(i_size)
+
+            def body(j, carry):
+                cols = pl.ds(pl.multiple_of(j * tile, tile), tile)
+                prod[p1, :, cols] = product3(
+                    both[:, :k_size], a[:, cols], ((1,), (0,))
+                )
+                return carry
+
+            lax.fori_loop(0, i_size // tile, body, 0)
+            core_copy(c1).start()
+
+        cy = c1 - 1
+        py = cy % 2
+
+        @pl.when(live(cy))
+        def _():
+            for n in range(len(bits)):
+                if n > 0:
+                    bit_copy(n, cy).start()
+                bit_copy(n, cy).wait()
+                add_into_kept(py, bit_in.at[n, py])
+            back_copy(cy).start()
 
         @pl.when(live(c1))
         def _():
@@ -331,26 +366,9 @@
             add_into_kept(p1, core_in.at[p1])
             bit_copy(0, c1).start()
 
-        @pl.when(live(c2))
-        def _():
-            tile = tile_of(x.shape[0])
-
-            def body(j, carry):
-                lines = pl.ds(pl.multiple_of(j * tile, tile), tile)
-                value = product3(hi[:, :i_size], lo[:, :i_size], x[lines], ((1,), (1,)))
-                part[c2 % z, :, :, lines] = value.reshape(z, chunk, tile)
-                return carry
-
-            lax.fori_loop(0, x.shape[0] // tile, body, 0)
-            for way in range(2):
-
-                @pl.when(places[way] == 0)
-                def _():
-                    rs_copy(way, 0, c2).start()
-
         return carry
 
-    lax.fori_loop(0, chunks + 2 * z - 1, step, 0)
+    lax.fori_loop(0, chunks + z + 1, step, 0)
     for c in range(chunks):
         give_copy(c).wait_recv()
         if c >= chunks - 2:
@@ -377,8 +395,7 @@
             pltpu.VMEM((k_size, i_size), f32),
             pltpu.VMEM((r_size, i_size), f32),
             pltpu.VMEM((ring, z, chunk, k_size), f32),
-            pltpu.VMEM((group, i_size if i_size >= k_size else k_size), bf16),
-            pltpu.VMEM((group, i_size if i_size >= k_size else k_size), bf16),
+            pltpu.VMEM((2 * group, max(i_size, k_size)), bf16),
             pltpu.VMEM((2, group, i_size), f32),
             pltpu.VMEM((2, share, i_size), f32),
             pltpu.VMEM((n_bits, 2, share, i_size), f32),

time: 402 us -> 405 us (level)
  no operation moved by 1% of the time
where the time goes in v4:
time: 405 us
  Pallas kernels  400 us (99%)
  local copies, waits for them, and re-layouts  4.99 us (1%)
    pallas_call x1, Pallas kernels, refresh(): pl.pallas_call(functools.partial(kernel, dims), out_shape=jax.ShapeDtypeS...  400 us

profile of v4, /device:TPU:0, one launch (start us, length us, event | category | flops | bytes accessed | tf_op | source)
XLA Modules:
  0.0 404.6 jit_solution(3813906284296576388)
XLA Ops:
  0.0 399.6 %shard_map.28 = f32[1024,896]{1,0:T(8,128)} custom-call(f32[1792,1792]{1,0:T(8,128)} %a_hbm.1, f32[1792,1792]{1,0:T(8,128)} %x_hbm.1), custom_call_target="tpu_custom_call" | custom-call | flops 78920024064 | bytes 40000000 | tf_op jit(solution)/shard_map/pallas_call | solution.py:389
  399.6 5.0 %copy.3 = f32[896,1024]{1,0:T(8,128)} copy(f32[896,1024]{0,1:T(8,128)} %bitcast.1) | data formatting | bytes 7340032 | tf_op jit(solution)/shard_map/transpose | solution.py:440
